TPU v7x, 32 devices: a whole 2x2x4 slice. The times are simulated.
32 devices in a mesh: wide: 4 (over y, x), narrow: 2 (over core), rep: 4 (over z).
Axes of the slice: x: 2, y: 2, z: 4, core: 2. Of those that a mesh axis runs over, the one named last changes fastest.
Arguments:
- queries: bfloat16 [4096, 2048], P(('rep', 'wide'), 'narrow'), parts along dimension 0, may hold values from -20 to 20
- key_rows: bfloat16 [4096, 512], P(('rep', 'wide'), 'narrow'), parts along dimension 0, may hold values from -20 to 20
- value_rows: bfloat16 [4096, 512], P(('rep', 'wide'), 'narrow'), parts along dimension 0, may hold values from -20 to 20
- residual: bfloat16 [4096, 4096], P(('rep', 'wide', 'narrow')), parts along dimension 0, may hold values from -9 to 9
- out_weight: bfloat16 [2048, 4096], P('narrow'), may hold values from -0.125 to 0.125
- norm_gain: bfloat16 [4096], replicated, may hold values from 0.099609375 to 1.8984375
- span_map: int32 [4], replicated, may hold values from 0 to 3, each once
- segments: int32 [16, 128], P(('rep', 'wide')), parts along dimension 0, may hold values from 0 to 8, as said below
- row_owner: int32 [4096, 1], P(('rep', 'wide', 'narrow')), parts along dimension 0, may hold values from 0 to 3; in each aligned block of 128 rows (0 to 127, 128 to 255, ...) at most 64 rows name the same one
Outputs:
- hidden: bfloat16 [4096, 4096], P(('rep', 'wide', 'narrow')), parts along dimension 0
- ffn_in: bfloat16 [16, 2, 4, 64, 4096], P(('rep', 'wide'), 'narrow'), parts along dimension 0
There are 4 independent parts, one for each index of `rep`. A program takes and returns all parts, laid end to end along the dimension named above; an argument that names none is the same for every part. Nothing has to cross between parts.
Inputs may be any that keep to these rules, and one draw needn't show every extreme that they name: `segments`: in each token block the short document numbers start at 0, never fall, and rise by at most one from a row to the next; short rows 0 and 1 lie in the same document; some token block reaches the largest number. `row_owner`: within each aligned block of 128 rows no owner is named by more than 64 rows; in some blocks an owner is named by exactly 64 rows.
All inputs are finite; a program needn't handle non-finite values.
Results may differ from a plain program's by a relative error of at most 0.012.
Values may be sent and summed in bfloat16 or wider, within the bound.
A program may use at most 64 MiB of HBM per device.

v0:
```python
import jax
import jax.numpy as jnp
from jax import lax
from jax.sharding import PartitionSpec as P

HEAD = 128
LONG_DEV = 128


def attend_block(
    partial_state, long_queries, key_block, value_block, key_pos, query_pos, score_scale
):
    running_max, weight_sum, weighted = partial_state
    scores = (
        jnp.einsum("qgjd,kgd->qgjk", long_queries, key_block, preferred_element_type=jnp.float32)
        * score_scale
    )
    visible = (key_pos[None, :] <= query_pos[:, None])[:, None, None, :]
    masked = jnp.where(visible, scores, -1e30)
    newest = jnp.maximum(running_max, jnp.max(masked, axis=-1))
    weights = jnp.where(visible, jnp.exp(masked - newest[..., None]), 0.0)
    factor = jnp.exp(running_max - newest)
    weight_sum = weight_sum * factor + jnp.sum(weights, axis=-1)
    weighted = weighted * factor[..., None] + jnp.einsum(
        "qgjk,kgd->qgjd",
        weights.astype(jnp.bfloat16),
        value_block,
        preferred_element_type=jnp.float32,
    )
    return (newest, weight_sum, weighted)


def rounded_term(attended, out_weight):
    product = jnp.dot(attended, out_weight, preferred_element_type=jnp.float32)
    return lax.optimization_barrier(product.astype(jnp.bfloat16)).astype(jnp.float32)


def on_device(
    queries, key_rows, value_rows, residual, out_weight, norm_gain, span_map, segments, row_owner
):
    wide_count = lax.axis_size("wide")
    narrow_count = lax.axis_size("narrow")
    wide_index = lax.axis_index("wide")
    local_heads = queries.shape[1] // HEAD
    local_kv = key_rows.shape[1] // HEAD
    group_size = local_heads // local_kv
    token_count = queries.shape[0]
    short_count = token_count - LONG_DEV
    score_scale = HEAD ** (-0.5)
    own_span = lax.dynamic_slice_in_dim(span_map, wide_index, 1, 0)[0]
    query_pos = own_span * LONG_DEV + jnp.arange(LONG_DEV, dtype=jnp.int32)
    long_queries = queries[:LONG_DEV].reshape(LONG_DEV, local_kv, group_size, HEAD)
    wide_ids = jnp.arange(wide_count, dtype=jnp.int32)
    start_state = (
        jnp.full((LONG_DEV, local_kv, group_size), -1e30, jnp.float32),
        jnp.zeros((LONG_DEV, local_kv, group_size), jnp.float32),
        jnp.zeros((LONG_DEV, local_kv, group_size, HEAD), jnp.float32),
    )
    key_piece = lax.all_gather(key_rows[:LONG_DEV], "wide", axis=0, tiled=True)
    value_piece = lax.all_gather(value_rows[:LONG_DEV], "wide", axis=0, tiled=True)
    row_count = key_piece.shape[0]
    key_index = jnp.arange(row_count, dtype=jnp.int32)
    holder = key_index // LONG_DEV
    span_of = jnp.sum(jnp.where(holder[:, None] == wide_ids[None, :], span_map[None, :], 0), axis=1)
    key_pos = span_of * LONG_DEV + key_index % LONG_DEV
    key_block = key_piece.reshape(row_count, local_kv, HEAD)
    value_block = value_piece.reshape(row_count, local_kv, HEAD)

    def advance(partial_state):
        if row_count > 512 and row_count % 512 == 0:
            splits = row_count // 512

            def advance_block(inner_state, sliced):
                return (
                    attend_block(
                        inner_state,
                        long_queries,
                        sliced[0],
                        sliced[1],
                        sliced[2],
                        query_pos,
                        score_scale,
                    ),
                    None,
                )

            finished, unused = lax.scan(
                advance_block,
                partial_state,
                (
                    key_block.reshape(splits, 512, local_kv, HEAD),
                    value_block.reshape(splits, 512, local_kv, HEAD),
                    key_pos.reshape(splits, 512),
                ),
            )
            return finished
        return attend_block(
            partial_state, long_queries, key_block, value_block, key_pos, query_pos, score_scale
        )

    running_max, weight_sum, weighted = advance(start_state)
    long_out = (
        (weighted / weight_sum[..., None])
        .astype(jnp.bfloat16)
        .reshape(LONG_DEV, local_heads * HEAD)
    )
    short_queries = queries[LONG_DEV:].reshape(short_count, local_kv, group_size, HEAD)
    short_keys = key_rows[LONG_DEV:].reshape(short_count, local_kv, HEAD)
    short_values = value_rows[LONG_DEV:].reshape(short_count, local_kv, HEAD)
    documents = segments[0]
    positions = jnp.arange(short_count, dtype=jnp.int32)
    visible = (
        (documents[None, :] == documents[:, None]) & (positions[None, :] <= positions[:, None])
    )[:, None, None, :]
    scores = (
        jnp.einsum("qgjd,kgd->qgjk", short_queries, short_keys, preferred_element_type=jnp.float32)
        * score_scale
    )
    masked = jnp.where(visible, scores, -1e30)
    row_max = jnp.max(masked, axis=-1, keepdims=True)
    weights = jnp.where(visible, jnp.exp(masked - row_max), 0.0)
    short_sum = jnp.sum(weights, axis=-1)
    mixed = jnp.einsum(
        "qgjk,kgd->qgjd",
        weights.astype(jnp.bfloat16),
        short_values,
        preferred_element_type=jnp.float32,
    )
    short_out = (
        (mixed / short_sum[..., None]).astype(jnp.bfloat16).reshape(short_count, local_heads * HEAD)
    )
    attended = jnp.concatenate([long_out, short_out], axis=0)
    rows_dev = token_count // narrow_count
    sliced = attended
    summed = lax.psum_scatter(
        rounded_term(sliced, out_weight).astype(jnp.bfloat16),
        "narrow",
        scatter_dimension=0,
        tiled=True,
    ).astype(jnp.float32)
    hidden = (residual.astype(jnp.float32) + summed).astype(jnp.bfloat16)
    widened = hidden.astype(jnp.float32)
    normed = (
        widened
        * lax.rsqrt(jnp.mean(widened * widened, axis=1, keepdims=True) + 1e-05)
        * norm_gain.astype(jnp.float32)
    ).astype(jnp.bfloat16)
    capacity = max(2, 2 * rows_dev // wide_count)
    owners = row_owner[:, 0]
    chosen = (owners[:, None] == wide_ids[None, :]).astype(jnp.int32)
    earlier = jnp.cumsum(chosen, axis=0) - chosen
    slot_index = jnp.sum(earlier * chosen, axis=1)
    target = owners * capacity + slot_index
    dispatch = (
        target[None, :] == jnp.arange(wide_count * capacity, dtype=jnp.int32)[:, None]
    ).astype(jnp.bfloat16)
    outgoing = jnp.dot(dispatch, normed, preferred_element_type=jnp.float32).astype(jnp.bfloat16)
    outgoing = outgoing.reshape(wide_count, 1, 1, capacity, normed.shape[1])
    arrived = lax.all_to_all(outgoing, "wide", split_axis=0, concat_axis=2, tiled=True)
    return (hidden, arrived)


def solution(mesh):
    placed = (
        P(("rep", "wide"), "narrow"),
        P(("rep", "wide"), "narrow"),
        P(("rep", "wide"), "narrow"),
        P(("rep", "wide", "narrow"), None),
        P("narrow", None),
        P(),
        P(),
        P(("rep", "wide"), None),
        P(("rep", "wide", "narrow"), None),
    )
    return jax.shard_map(
        on_device,
        mesh=mesh,
        in_specs=placed,
        out_specs=(
            P(("rep", "wide", "narrow"), None),
            P(("rep", "wide"), "narrow", None, None, None),
        ),
        check_vma=False,
    )
```

profile of v0, /device:TPU:0, one launch (start us, length us, event | category | flops | bytes accessed | tf_op | source)
XLA Modules:
  0.0 96.0 jit_solution(12283998246947713480)
XLA Ops:
  7.2 0.0 copy-start.2
  7.2 0.0 reduce-scatter.2.cloned.1.call-start
  7.2 1.3 %dynamic_slice.3 = s32[1]{0:T(128)} dynamic-slice(s32[4]{0:T(128)} %param.15, s32[]{:T(128)S(6)} %select_n.44), dynamic_slice_sizes={1} | dynamic-slice | bytes 12 | tf_op jit(solution)/shard_map/dynamic_slice | solution.py:50
  9.2 0.7 select_reduce_fusion.1
  9.9 0.8 fusion.32
  10.8 0.9 fusion.51
  11.6 0.1 copy.65
  11.8 0.1 copy.67
  11.9 0.9 fusion.52
  12.8 0.1 copy.50
  12.9 10.4 %all_gather.7 = bf16[512,256]{1,0:T(8,128)(2,1)S(1)} all-gather(bf16[128,256]{1,0:T(8,128)(2,1)S(1)} %get-tuple-element.8), channel_id=1, replica_groups=mesh['wide'=4,'narrow'=2,'rep'=4] {'wide'}, dimensions={0}, use_global_device_ids=true | all-gather | bytes 327680 | tf_op jit(solution)/shard_map/all_gather | solution.py:60
  23.3 0.1 copy.44
  23.5 9.0 %all_gather.6 = bf16[512,256]{0,1:T(8,128)(2,1)S(1)} all-gather(bf16[128,256]{0,1:T(8,128)(2,1)S(1)} %copy.65), channel_id=1, replica_groups=mesh['wide'=4,'narrow'=2,'rep'=4] {'wide'}, dimensions={0}, use_global_device_ids=true | all-gather | bytes 327680 | tf_op jit(solution)/shard_map/all_gather | solution.py:59
  32.5 0.0 copy-done.2
  32.5 0.2 copy.66
  32.7 0.2 copy.68
  32.9 0.3 fusion.15
  33.1 0.9 fusion
  34.1 0.1 broadcast_compare_fusion
  34.2 0.5 fusion.5
  34.7 0.0 copy-start.3
  34.8 0.5 fusion.6
  35.3 0.6 exponential_multiply_fusion
  35.9 0.0 copy-done.3
  35.9 1.3 %fusion.17 = bf16[128,2,4,128]{0,3,2,1:T(8,128)(2,1)S(1)} fusion(f32[128,2,4,128]{0,3,2,1:T(8,128)} %fusion, bf16[128,2,128,1]{0,2,3,1:T(8,128)(2,1)S(1)} %bitcast.79, f32[128,2,4,128]{0,3,2,1:T(8,128)S(1)} %fusion.15, pred[128,128]{0,1:T(8,128)(4,1)S(1)} %fusion.32), kind=kOutput, calls=%fused_computation.27 | convolution fusion | flops 34210944 | bytes 1392640 | tf_op jit(solution)/shard_map/qgjk,kgd->qgjd/dot_general | solution.py:123
  37.2 1.4 %fusion.16 = bf16[128,2,4,128]{0,3,2,1:T(8,128)(2,1)S(1)} fusion(bf16[512,2,128,1]{0,2,3,1:T(8,128)(2,1)S(1)} %bitcast.75, f32[2,512,128,4]{2,1,3,0:T(8,128)S(1)} %get-tuple-element.13, f32[128,2,4]{0,2,1:T(4,128)} %copy-done.3, pred[128,512]{0,1:T(8,128)(4,1)S(1)} %broadcast_compare_fusion, f32[128,2,4]{0,2,1:T(4,128)} %get-tuple-element.11, ...), kind=kOutput, calls=%fused_computation.26 | convolution fusion | flops 137232384 | bytes 2699264 | tf_op jit(solution)/shard_map/qgjk,kgd->qgjd/dot_general | solution.py:24
  38.6 7.1 %convolution_convert_fusion.1 = bf16[256,4096]{1,0:T(8,128)(2,1)} fusion(bf16[1024,4096]{1,0:T(8,128)(2,1)} %param.13, bf16[128,1024]{0,1:T(8,128)(2,1)S(1)} %bitcast.77, bf16[128,1024]{0,1:T(8,128)(2,1)S(1)} %bitcast.78), kind=kOutput, calls=%fused_computation.3 | convolution fusion | flops 2149580800 | bytes 11010048 | tf_op jit(solution)/shard_map/dot_general | solution.py:34
  45.7 0.0 copy-start.4
  45.7 0.0 copy-start.5
  45.7 0.0 copy-start.1
  45.7 0.0 reduce-scatter.2.cloned.1.call-update
  45.7 0.7 copy-done.4
  46.4 0.0 copy-done.5
  46.4 0.1 fusion.31
  46.5 0.2 reduce_window_sum.11
  46.6 0.2 select_reduce_fusion
  46.8 8.9 %reduce-scatter.2.cloned.1.call-done = bf16[128,4096]{1,0:T(8,128)(2,1)} async-done(((bf16[256,4096]{1,0:T(8,128)(2,1)}), bf16[128,4096]{1,0:T(8,128)(2,1)}) %reduce-scatter.2.cloned.1.call-update) | async-done | bytes 1048592 | tf_op jit(solution)/shard_map/reduce_scatter | solution.py:135
  55.7 0.0 copy-done.1
  55.7 1.7 %fusion.2 = (f32[128]{0:T(128)S(1)}, bf16[128,4096]{1,0:T(8,128)(2,1)S(1)}) fusion(bf16[128,4096]{1,0:T(8,128)(2,1)} %reduce-scatter.2.cloned.1.call-done, bf16[128,4096]{1,0:T(8,128)(2,1)S(1)} %copy-done.1), kind=kLoop, calls=%fused_computation.6 | loop fusion | flops 3669888 | bytes 3146240 | tf_op jit(solution)/shard_map/reduce_sum | solution.py:145
  57.4 0.0 copy-start
  57.4 0.8 convolution_convert_fusion
  58.2 29.5 %all_to_all.12 = bf16[4,1,1,64,4096]{4,3,2,1,0:T(8,128)(2,1)S(1)} all-to-all(bf16[4,1,1,64,4096]{4,3,2,1,0:T(8,128)(2,1)S(1)} %bitcast.70), channel_id=1, replica_groups=mesh['wide'=4,'narrow'=2,'rep'=4] {'wide'}, dimensions={0} | all-to-all | bytes 4194304 | tf_op jit(solution)/shard_map/all_to_all | solution.py:159
  87.8 0.0 copy-done
  87.8 1.3 %copy.70 = bf16[1,1,4,64,4096]{4,3,2,1,0:T(8,128)(2,1)} copy(bf16[1,1,4,64,4096]{4,3,2,1,0:T(8,128)(2,1)S(1)} %bitcast.71) | data formatting | bytes 4194304
  (8 shorter events, 0.1 us)
Async XLA Ops:
  7.2 25.3 %copy-start.2 = (bf16[256,1024]{1,0:T(8,128)(2,1)S(1)}, bf16[256,1024]{1,0:T(8,128)(2,1)}, u32[]{:S(2)}) copy-start(bf16[256,1024]{1,0:T(8,128)(2,1)} %param.9) | copy-start | bytes 1572868
  7.2 48.6 %reduce-scatter.2.cloned.1.call-start = ((), (), s32[]{:S(2)}) async-start(), calls=%async_computation.2 | async-start | bytes 3145728 | tf_op jit(solution)/shard_map/reduce_scatter | solution.py:135
  34.7 1.1 %copy-start.3 = (f32[128,2,4]{0,2,1:T(4,128)}, f32[128,2,4]{0,2,1:T(4,128)S(1)}, u32[]{:S(2)}) copy-start(f32[128,2,4]{0,2,1:T(4,128)S(1)} %broadcast_maximum_fusion) | copy-start | bytes 12292
  45.7 0.7 copy-start.4
  45.7 0.7 copy-start.5
  45.7 10.1 %copy-start.1 = (bf16[128,4096]{1,0:T(8,128)(2,1)S(1)}, bf16[128,4096]{1,0:T(8,128)(2,1)}, u32[]{:S(2)}) copy-start(bf16[128,4096]{1,0:T(8,128)(2,1)} %param.12) | copy-start | bytes 3145732
  57.4 30.4 %copy-start = (bf16[128,4096]{1,0:T(8,128)(2,1)}, bf16[128,4096]{1,0:T(8,128)(2,1)S(1)}, u32[]{:S(2)}) copy-start(bf16[128,4096]{1,0:T(8,128)(2,1)S(1)} %get-tuple-element.16) | copy-start | bytes 3145732
Sparse Core Ops, SparseCore 0:
  45.8 9.8 reduce-scatter.1
where the time goes:
time: 96.5 us; the launch traced here: 96 us
  blocking collectives  49 us (51%)
  between operations  14.9 us (15%)
  matrix products  11.3 us (12%)
  waiting for transfers between devices  8.92 us (9%)
  local copies, waits for them, and re-layouts  5.93 us (6%)
  other arithmetic  5.89 us (6%)
    all_to_all x1, blocking collectives, on_device(): lax.all_to_all(outgoing, 'wide', split_axis=0, concat_axis=2, tiled=True)  29.5 us
    all_gather x1, blocking collectives, on_device(): lax.all_gather(value_rows[:LONG_DEV], 'wide', axis=0, tiled=True)  10.4 us
    all_gather x1, blocking collectives, on_device(): key_piece = lax.all_gather(key_rows[:LONG_DEV], 'wide', axis=0, tiled=True)  8.97 us
    reduce_scatter x1, waiting for transfers between devices, on_device(): lax.psum_scatter(rounded_term(sliced, out_weight).astype(jnp.bfloat16), '...  8.9 us
    dot_general x1, matrix products, rounded_term(): product = jnp.dot(attended, out_weight, preferred_element_type=jnp.float32)  7.08 us
    unnamed x17, local copies, waits for them, and re-layouts  2.58 us
  transfers between devices with their start and end apart: 1, of which 1 were waited for; matrix products, arithmetic and copies ran while one was open for 0% of the time, Pallas kernels for 0%

commit v1 on v0

--- a/solution.py
+++ b/solution.py
@@ -1,6 +1,10 @@
+import functools
+
 import jax
 import jax.numpy as jnp
 from jax import lax
+from jax.experimental import pallas as pl
+from jax.experimental.pallas import tpu as pltpu
 from jax.sharding import PartitionSpec as P
 
 HEAD = 128
@@ -35,7 +39,7 @@
     return lax.optimization_barrier(product.astype(jnp.bfloat16)).astype(jnp.float32)
 
 
-def on_device(
+def general_on_device(
     queries, key_rows, value_rows, residual, out_weight, norm_gain, span_map, segments, row_owner
 ):
     wide_count = lax.axis_size("wide")
@@ -160,6 +164,370 @@
     return (hidden, arrived)
 
 
+PIECES = 8
+SENDS = 4
+MESH = pl.DeviceIdType.MESH
+
+
+def attend_heads(q_buf, keys, values, visible, rows, out_buf, lane, local_kv, group_size):
+    score_scale = HEAD ** (-0.5)
+    count = rows.stop - rows.start
+    tiled = jnp.concatenate([visible] * group_size, axis=0)
+    for g in range(local_kv):
+        heads = [g * group_size + j for j in range(group_size)]
+        stacked = jnp.concatenate([q_buf[rows, h * HEAD : (h + 1) * HEAD] for h in heads], axis=0)
+        scores = (
+            lax.dot_general(
+                stacked, keys(g), (((1,), (1,)), ((), ())), preferred_element_type=jnp.float32
+            )
+            * score_scale
+        )
+        masked = jnp.where(tiled, scores, -1e30)
+        weights = jnp.exp(masked - jnp.max(masked, axis=1, keepdims=True))
+        total = jnp.sum(weights, axis=1, keepdims=True)
+        mixed = jnp.dot(
+            weights.astype(jnp.bfloat16), values(g), preferred_element_type=jnp.float32
+        )
+        mixed = (mixed / total).astype(jnp.bfloat16)
+        for j, h in enumerate(heads):
+            out_buf[lane, :, h * HEAD : (h + 1) * HEAD] = mixed[j * count : (j + 1) * count]
+
+
+def fused_kernel(
+    sizes,
+    span_ref,
+    seg_ref,
+    owner_ref,
+    q_hbm,
+    k_hbm,
+    v_hbm,
+    res_hbm,
+    w_hbm,
+    gain_ref,
+    hidden_hbm,
+    ffn_hbm,
+    q_buf,
+    ks_buf,
+    vs_buf,
+    k_buf,
+    v_buf,
+    w_buf,
+    res_buf,
+    att_buf,
+    part_buf,
+    recv_buf,
+    hid_buf,
+    out_buf,
+    in_sem,
+    w_sem,
+    k_send,
+    k_recv,
+    v_send,
+    v_recv,
+    p_send,
+    p_recv,
+    o_send,
+    o_recv,
+    own_sem,
+    hid_sem,
+):
+    wide_count, capacity, local_kv, group_size = sizes
+    rows, model = res_hbm.shape
+    piece = model // PIECES
+    span = model // SENDS
+    me = lax.axis_index("wide")
+    lane = lax.axis_index("narrow")
+    other = 1 - lane
+    peers = [lax.rem(me + k, wide_count) for k in range(1, wide_count)]
+    long_rows, short_rows = slice(0, rows), slice(rows, 2 * rows)
+
+    loads = [
+        pltpu.make_async_copy(q_hbm, q_buf, in_sem.at[0]),
+        pltpu.make_async_copy(k_hbm.at[pl.ds(rows, rows)], ks_buf, in_sem.at[1]),
+        pltpu.make_async_copy(v_hbm.at[pl.ds(rows, rows)], vs_buf, in_sem.at[2]),
+    ]
+    late_loads = [
+        pltpu.make_async_copy(k_hbm.at[pl.ds(0, rows)], k_buf.at[me], in_sem.at[3]),
+        pltpu.make_async_copy(v_hbm.at[pl.ds(0, rows)], v_buf.at[me], in_sem.at[4]),
+    ]
+    res_load = pltpu.make_async_copy(res_hbm, res_buf, in_sem.at[5])
+    w_loads = [
+        pltpu.make_async_copy(
+            w_hbm.at[:, pl.ds(c * piece, piece)], w_buf.at[c], w_sem.at[c]
+        )
+        for c in range(PIECES)
+    ]
+    for load in loads + w_loads + [res_load] + late_loads:
+        load.start()
+
+    barrier = pltpu.get_barrier_semaphore()
+    for peer in peers:
+        pl.semaphore_signal(barrier, inc=1, device_id={"wide": peer}, device_id_type=MESH)
+    pl.semaphore_signal(barrier, inc=1, device_id={"narrow": other}, device_id_type=MESH)
+    pl.semaphore_wait(barrier, wide_count)
+
+    def kv_copy(source, peer):
+        return [
+            pltpu.make_async_remote_copy(
+                src_ref=hbm.at[pl.ds(0, rows)],
+                dst_ref=buf.at[source],
+                send_sem=send.at[peer],
+                recv_sem=recv.at[source],
+                device_id={"wide": peer},
+                device_id_type=MESH,
+            )
+            for hbm, buf, send, recv in (
+                (k_hbm, k_buf, k_send, k_recv),
+                (v_hbm, v_buf, v_send, v_recv),
+            )
+        ]
+
+    for peer in peers:
+        for copy in kv_copy(me, peer):
+            copy.start()
+
+    row_id = lax.broadcasted_iota(jnp.int32, (rows, rows), 0)
+    col_id = lax.broadcasted_iota(jnp.int32, (rows, rows), 1)
+
+    owner_down = jnp.broadcast_to(owner_ref[...], (rows, rows)).astype(jnp.float32)
+    owner_across = owner_down.T
+    same = jnp.where((owner_down == owner_across) & (row_id < col_id), 1.0, 0.0)
+    slot = jnp.sum(same, axis=0, keepdims=True)
+    target = (owner_across[0:1] * capacity + slot).astype(jnp.int32)
+    slots = lax.broadcasted_iota(jnp.int32, (wide_count * capacity, rows), 0)
+    dispatch = jnp.where(slots == target, 1.0, 0.0).astype(jnp.bfloat16)
+
+    def part_copy(c, phase):
+        return pltpu.make_async_remote_copy(
+            src_ref=part_buf.at[phase, c],
+            dst_ref=recv_buf.at[c],
+            send_sem=p_send.at[c],
+            recv_sem=p_recv.at[c],
+            device_id={"narrow": other},
+            device_id_type=MESH,
+        )
+
+    def project(phase, first):
+        def step(c, carry):
+            if first:
+                pltpu.make_async_copy(
+                    w_hbm.at[:, pl.ds(pl.multiple_of(c * piece, piece), piece)],
+                    w_buf.at[c],
+                    w_sem.at[c],
+                ).wait()
+            product = jnp.dot(att_buf[phase], w_buf[c], preferred_element_type=jnp.float32)
+            part_buf[phase, c] = product.astype(jnp.bfloat16)
+
+            @pl.when(lane != phase)
+            def _():
+                part_copy(c, phase).start()
+
+            return carry
+
+        lax.fori_loop(0, PIECES, step, 0)
+
+    def out_copy(c, source, peer):
+        return pltpu.make_async_remote_copy(
+            src_ref=out_buf.at[c, peer],
+            dst_ref=ffn_hbm.at[source, :, pl.ds(pl.multiple_of(c * span, span), span)],
+            send_sem=o_send.at[c, peer],
+            recv_sem=o_recv.at[c, source],
+            device_id={"wide": peer},
+            device_id_type=MESH,
+        )
+
+    def own_copy(c):
+        return pltpu.make_async_copy(
+            out_buf.at[c, me],
+            ffn_hbm.at[me, :, pl.ds(pl.multiple_of(c * span, span), span)],
+            own_sem.at[c],
+        )
+
+    hid_copy = pltpu.make_async_copy(hid_buf, hidden_hbm, hid_sem.at[0])
+
+    def finish(phase):
+        res_load.wait()
+
+        def add_piece(c, squares):
+            part_copy(c, phase).wait_recv()
+            cols = pl.ds(pl.multiple_of(c * piece, piece), piece)
+            summed = part_buf[phase, c].astype(jnp.float32) + recv_buf[c].astype(jnp.float32)
+            hidden = (res_buf[:, cols].astype(jnp.float32) + summed).astype(jnp.bfloat16)
+            hid_buf[:, cols] = hidden
+            widened = hidden.astype(jnp.float32)
+            return squares + jnp.sum(widened * widened, axis=1, keepdims=True)
+
+        squares = lax.fori_loop(0, PIECES, add_piece, jnp.zeros((rows, 1), jnp.float32))
+        hid_copy.start()
+        factor = lax.rsqrt(squares / model + 1e-05)
+
+        def send_piece(c, carry):
+            cols = pl.ds(pl.multiple_of(c * span, span), span)
+            normed = (
+                hid_buf[:, cols].astype(jnp.float32) * factor * gain_ref[:, cols].astype(jnp.float32)
+            ).astype(jnp.bfloat16)
+            outgoing = jnp.dot(dispatch, normed, preferred_element_type=jnp.float32)
+            out_buf[c] = outgoing.astype(jnp.bfloat16).reshape(wide_count, capacity, span)
+            for peer in peers:
+                out_copy(c, me, peer).start()
+            own_copy(c).start()
+            return carry
+
+        lax.fori_loop(0, SENDS, send_piece, 0)
+
+    for load in loads:
+        load.wait()
+    seg_across = jnp.broadcast_to(seg_ref[...], (rows, rows)).astype(jnp.float32)
+    short_visible = (seg_across == seg_across.T) & (col_id <= row_id)
+    attend_heads(
+        q_buf,
+        lambda g: ks_buf[:, g * HEAD : (g + 1) * HEAD],
+        lambda g: vs_buf[:, g * HEAD : (g + 1) * HEAD],
+        short_visible,
+        short_rows,
+        att_buf,
+        1,
+        local_kv,
+        group_size,
+    )
+    project(1, True)
+
+    @pl.when(lane == 1)
+    def _():
+        finish(1)
+
+    for load in late_loads:
+        load.wait()
+    for peer in peers:
+        for copy in kv_copy(peer, peer):
+            copy.wait_recv()
+    own_span = span_ref[me]
+    long_visible = jnp.concatenate(
+        [
+            (span_ref[b] * rows + col_id) <= (own_span * rows + row_id)
+            for b in range(wide_count)
+        ],
+        axis=1,
+    )
+    attend_heads(
+        q_buf,
+        lambda g: k_buf[:, :, g * HEAD : (g + 1) * HEAD].reshape(wide_count * rows, HEAD),
+        lambda g: v_buf[:, :, g * HEAD : (g + 1) * HEAD].reshape(wide_count * rows, HEAD),
+        long_visible,
+        long_rows,
+        att_buf,
+        0,
+        local_kv,
+        group_size,
+    )
+    project(0, False)
+
+    @pl.when(lane == 0)
+    def _():
+        finish(0)
+
+    for peer in peers:
+        for copy in kv_copy(me, peer):
+            copy.wait_send()
+
+    def drain_parts(c, carry):
+        part_copy(c, 0).wait_send()
+        return carry
+
+    lax.fori_loop(0, PIECES, drain_parts, 0)
+
+    def drain_sends(c, carry):
+        for peer in peers:
+            out_copy(c, me, peer).wait_send()
+            out_copy(c, peer, peer).wait_recv()
+        own_copy(c).wait()
+        return carry
+
+    lax.fori_loop(0, SENDS, drain_sends, 0)
+    hid_copy.wait()
+
+
+def fused_on_device(
+    queries, key_rows, value_rows, residual, out_weight, norm_gain, span_map, segments, row_owner
+):
+    wide_count = lax.axis_size("wide")
+    local_heads = queries.shape[1] // HEAD
+    local_kv = key_rows.shape[1] // HEAD
+    rows, model = residual.shape
+    capacity = max(2, 2 * rows // wide_count)
+    sizes = (wide_count, capacity, local_kv, local_heads // local_kv)
+    bf16 = jnp.bfloat16
+    dma = pltpu.SemaphoreType.DMA
+    any_spec = pl.BlockSpec(memory_space=pl.ANY)
+    vmem_spec = pl.BlockSpec(memory_space=pltpu.VMEM)
+    piece, span = model // PIECES, model // SENDS
+    hidden, arrived = pl.pallas_call(
+        functools.partial(fused_kernel, sizes),
+        out_shape=(
+            jax.ShapeDtypeStruct((rows, model), bf16),
+            jax.ShapeDtypeStruct((wide_count, capacity, model), bf16),
+        ),
+        in_specs=[pl.BlockSpec(memory_space=pltpu.SMEM), vmem_spec, vmem_spec]
+        + [any_spec] * 5
+        + [vmem_spec],
+        out_specs=(any_spec, any_spec),
+        scratch_shapes=[
+            pltpu.VMEM(queries.shape, bf16),
+            pltpu.VMEM((rows, key_rows.shape[1]), bf16),
+            pltpu.VMEM((rows, key_rows.shape[1]), bf16),
+            pltpu.VMEM((wide_count, rows, key_rows.shape[1]), bf16),
+            pltpu.VMEM((wide_count, rows, key_rows.shape[1]), bf16),
+            pltpu.VMEM((PIECES, out_weight.shape[0], piece), bf16),
+            pltpu.VMEM((rows, model), bf16),
+            pltpu.VMEM((2, rows, queries.shape[1]), bf16),
+            pltpu.VMEM((2, PIECES, rows, piece), bf16),
+            pltpu.VMEM((PIECES, rows, piece), bf16),
+            pltpu.VMEM((rows, model), bf16),
+            pltpu.VMEM((SENDS, wide_count, capacity, span), bf16),
+            dma((6,)),
+            dma((PIECES,)),
+            dma((wide_count,)),
+            dma((wide_count,)),
+            dma((wide_count,)),
+            dma((wide_count,)),
+            dma((PIECES,)),
+            dma((PIECES,)),
+            dma((SENDS, wide_count)),
+            dma((SENDS, wide_count)),
+            dma((SENDS,)),
+            dma((1,)),
+        ],
+        compiler_params=pltpu.CompilerParams(
+            collective_id=0, has_side_effects=True, vmem_limit_bytes=56 * 1024 * 1024
+        ),
+    )(
+        span_map,
+        segments,
+        row_owner,
+        queries,
+        key_rows,
+        value_rows,
+        residual,
+        out_weight,
+        norm_gain.reshape(1, model),
+    )
+    return hidden, arrived.reshape(1, 1, wide_count, capacity, model)
+
+
+def on_device(*args):
+    queries, residual = args[0], args[3]
+    rows, model = residual.shape
+    wide_count = lax.axis_size("wide")
+    fits = (
+        lax.axis_size("narrow") == 2
+        and rows == LONG_DEV
+        and queries.shape[0] == 2 * LONG_DEV
+        and (2 * rows) % (16 * wide_count) == 0
+        and model % (PIECES * HEAD) == 0
+    )
+    return (fused_on_device if fits else general_on_device)(*args)
+
+
 def solution(mesh):
     placed = (
         P(("rep", "wide"), "narrow"),

time: 96.5 us -> 43 us (0.45)
  blocking collectives: 49 us -> 0 us
  Pallas kernels: 0 us -> 35.6 us
  between operations: 14.9 us -> 0.65 us
  matrix products: 11.3 us -> 0 us
  waiting for transfers between devices: 8.92 us -> 0 us
  other arithmetic: 5.89 us -> 0 us
    pallas_call x0 -> x1, Pallas kernels: none -> 35.6 us  [fused_on_device(): pl.pallas_call(functools.partial(fused_kernel, sizes), out_shape=(jax.Sha...]
    all_to_all x1 -> x0, blocking collectives: 29.5 us -> none  [on_device(): lax.all_to_all(outgoing, 'wide', split_axis=0, concat_axis=2, tiled=True)]
    all_gather x2 -> x0, blocking collectives: 19.4 us -> none  [the longest x1 10.4 us: on_device(): lax.all_gather(value_rows[:LONG_DEV], 'wide', axis=0, tiled=True)]
    dot_general x6 -> x0, matrix products: 11.3 us -> none  [the longest x1 7.08 us: rounded_term(): product = jnp.dot(attended, out_weight, preferred_element_type=jnp.float32)]
    reduce_scatter x1 -> x0, waiting for transfers between devices: 8.9 us -> none  [on_device(): lax.psum_scatter(rounded_term(sliced, out_weight).astype(jnp.bfloat16), '...]
    reduce_sum x4 -> x0, other arithmetic: 3.11 us -> none  [the longest x1 1.68 us: on_device(): jnp.mean(widened * widened, axis=1, keepdims=True) + 1e-05]
    unnamed x17 -> x5, local copies, waits for them, and re-layouts: 2.58 us -> 5.15 us
    slice x4 -> x0, local copies, waits for them, and re-layouts: 1.92 us -> none  [the longest x1 0.89 us: on_device(): value_rows[:LONG_DEV]]
  transfers between devices with their start and end apart: 1 -> 0, of which waited for: 1 -> 0; matrix products, arithmetic and copies ran while one was open for 0% -> 0% of each run, Pallas kernels for 0% -> 0%
where the time goes in v1:
time: 43 us; the launch traced here: 42.7 us
  Pallas kernels  35.6 us (83%)
  local copies, waits for them, and re-layouts  6.46 us (15%)
  between operations  0.65 us (2%)
    pallas_call x1, Pallas kernels, fused_on_device(): pl.pallas_call(functools.partial(fused_kernel, sizes), out_shape=(jax.Sha...  35.6 us
    unnamed x5, local copies, waits for them, and re-layouts  5.15 us
    reshape x1, local copies, waits for them, and re-layouts, fused_on_device(): norm_gain.reshape(1, model)  1.31 us

profile of v1, /device:TPU:0, one launch (start us, length us, event | category | flops | bytes accessed | tf_op | source)
XLA Modules:
  0.0 42.7 jit_solution(11219189324908289174)
XLA Ops:
  0.6 1.3 %reshape.10.gain_ref = bf16[1,4096]{1,0:T(2,128)(2,1)} reshape(bf16[4096]{0:T(1024)(128)(2,1)} %param.14) | data formatting | bytes 16384 | tf_op jit(solution)/shard_map/reshape | solution.py:512
  1.9 1.4 %copy.11.owner_ref = s32[128,1]{1,0:T(8,128)} copy(s32[128,1]{0,1:T(1,128)} %param.17) | data formatting | bytes 1024 | tf_op args[8]
  3.3 35.6 %shard_map.104 = (bf16[128,4096]{1,0:T(8,128)(2,1)}, bf16[4,64,4096]{2,1,0:T(8,128)(2,1)}) custom-call(s32[4]{0:T(128)} %span_ref.1, s32[1,128]{1,0:T(1,128)} %seg_ref.1, s32[128,1]{1,0:T(8,128)} %copy.11.owner_ref, bf16[256,1024]{1,0:T(8,128)(2,1)} %q_hbm.1, bf16[256,256]{1,0:T(8,128)(2,1)} %k_hbm.1, bf16[256,256]{1,0:T(8,128)(2,1)} %v_hbm.1, ...), custom_call_target="tpu_custom_call" | custom-call | tf_op jit(solution)/shard_map/pallas_call | solution.py:464
  38.9 0.0 copy-start
  39.0 2.4 %copy.14 = bf16[128,4096]{1,0:T(8,128)(2,1)} copy(bf16[128,4096]{1,0:T(8,128)(2,1)} %get-tuple-element.8) | data formatting | bytes 2097152
  41.4 0.0 copy-done
  41.4 1.3 %copy.15 = bf16[1,1,4,64,4096]{4,3,2,1,0:T(8,128)(2,1)} copy(bf16[1,1,4,64,4096]{4,3,2,1,0:T(8,128)(2,1)S(1)} %bitcast.1) | data formatting | bytes 4194304
Async XLA Ops:
  38.9 2.4 %copy-start = (bf16[4,64,4096]{2,1,0:T(8,128)(2,1)S(1)}, bf16[4,64,4096]{2,1,0:T(8,128)(2,1)}, u32[]{:S(2)}) copy-start(bf16[4,64,4096]{2,1,0:T(8,128)(2,1)} %get-tuple-element.5) | copy-start | bytes 6291460

commit v2 on v1

--- a/solution.py
+++ b/solution.py
@@ -204,8 +204,8 @@
     res_hbm,
     w_hbm,
     gain_ref,
-    hidden_hbm,
-    ffn_hbm,
+    hidden_ref,
+    ffn_ref,
     q_buf,
     ks_buf,
     vs_buf,
@@ -216,7 +216,6 @@
     att_buf,
     part_buf,
     recv_buf,
-    hid_buf,
     out_buf,
     in_sem,
     w_sem,
@@ -229,7 +228,6 @@
     o_send,
     o_recv,
     own_sem,
-    hid_sem,
 ):
     wide_count, capacity, local_kv, group_size = sizes
     rows, model = res_hbm.shape
@@ -289,8 +287,8 @@
     row_id = lax.broadcasted_iota(jnp.int32, (rows, rows), 0)
     col_id = lax.broadcasted_iota(jnp.int32, (rows, rows), 1)
 
-    owner_down = jnp.broadcast_to(owner_ref[...], (rows, rows)).astype(jnp.float32)
-    owner_across = owner_down.T
+    owner_across = jnp.broadcast_to(owner_ref[...], (rows, rows)).astype(jnp.float32)
+    owner_down = owner_across.T
     same = jnp.where((owner_down == owner_across) & (row_id < col_id), 1.0, 0.0)
     slot = jnp.sum(same, axis=0, keepdims=True)
     target = (owner_across[0:1] * capacity + slot).astype(jnp.int32)
@@ -307,29 +305,21 @@
             device_id_type=MESH,
         )
 
-    def project(phase, first):
-        def step(c, carry):
-            if first:
-                pltpu.make_async_copy(
-                    w_hbm.at[:, pl.ds(pl.multiple_of(c * piece, piece), piece)],
-                    w_buf.at[c],
-                    w_sem.at[c],
-                ).wait()
-            product = jnp.dot(att_buf[phase], w_buf[c], preferred_element_type=jnp.float32)
-            part_buf[phase, c] = product.astype(jnp.bfloat16)
-
-            @pl.when(lane != phase)
-            def _():
-                part_copy(c, phase).start()
-
-            return carry
-
-        lax.fori_loop(0, PIECES, step, 0)
+    def project(phase, c):
+        if phase == 1:
+            w_loads[c].wait()
+        product = jnp.dot(att_buf[phase], w_buf[c], preferred_element_type=jnp.float32)
+        part_buf[phase, c] = product.astype(jnp.bfloat16)
+
+    def lend(phase):
+        for c in range(PIECES):
+            project(phase, c)
+            part_copy(c, phase).start()
 
     def out_copy(c, source, peer):
         return pltpu.make_async_remote_copy(
             src_ref=out_buf.at[c, peer],
-            dst_ref=ffn_hbm.at[source, :, pl.ds(pl.multiple_of(c * span, span), span)],
+            dst_ref=ffn_ref.at[source, :, pl.ds(c * span, span)],
             send_sem=o_send.at[c, peer],
             recv_sem=o_recv.at[c, source],
             device_id={"wide": peer},
@@ -339,41 +329,47 @@
     def own_copy(c):
         return pltpu.make_async_copy(
             out_buf.at[c, me],
-            ffn_hbm.at[me, :, pl.ds(pl.multiple_of(c * span, span), span)],
+            ffn_ref.at[me, :, pl.ds(c * span, span)],
             own_sem.at[c],
         )
-
-    hid_copy = pltpu.make_async_copy(hid_buf, hidden_hbm, hid_sem.at[0])
 
     def finish(phase):
         res_load.wait()
-
-        def add_piece(c, squares):
+        squares = jnp.zeros((rows, 1), jnp.float32)
+        for step in range(PIECES + 1):
+            if step < PIECES:
+                project(phase, step)
+            if step == 0:
+                continue
+            c = step - 1
             part_copy(c, phase).wait_recv()
-            cols = pl.ds(pl.multiple_of(c * piece, piece), piece)
+            cols = slice(c * piece, (c + 1) * piece)
             summed = part_buf[phase, c].astype(jnp.float32) + recv_buf[c].astype(jnp.float32)
             hidden = (res_buf[:, cols].astype(jnp.float32) + summed).astype(jnp.bfloat16)
-            hid_buf[:, cols] = hidden
+            hidden_ref[:, cols] = hidden
             widened = hidden.astype(jnp.float32)
-            return squares + jnp.sum(widened * widened, axis=1, keepdims=True)
-
-        squares = lax.fori_loop(0, PIECES, add_piece, jnp.zeros((rows, 1), jnp.float32))
-        hid_copy.start()
+            squares += jnp.sum(widened * widened, axis=1, keepdims=True)
         factor = lax.rsqrt(squares / model + 1e-05)
-
-        def send_piece(c, carry):
-            cols = pl.ds(pl.multiple_of(c * span, span), span)
-            normed = (
-                hid_buf[:, cols].astype(jnp.float32) * factor * gain_ref[:, cols].astype(jnp.float32)
-            ).astype(jnp.bfloat16)
+        lines = span // HEAD
+        for c in range(SENDS):
+            cols = slice(c * span, (c + 1) * span)
+            gains = gain_ref[c * lines : (c + 1) * lines, :].astype(jnp.float32)
+            gain = jnp.concatenate([gains[i : i + 1] for i in range(lines)], axis=1)
+            normed = (hidden_ref[:, cols].astype(jnp.float32) * factor * gain).astype(jnp.bfloat16)
             outgoing = jnp.dot(dispatch, normed, preferred_element_type=jnp.float32)
             out_buf[c] = outgoing.astype(jnp.bfloat16).reshape(wide_count, capacity, span)
             for peer in peers:
                 out_copy(c, me, peer).start()
             own_copy(c).start()
-            return carry
-
-        lax.fori_loop(0, SENDS, send_piece, 0)
+
+    def both(phase):
+        @pl.when(lane == phase)
+        def _():
+            finish(phase)
+
+        @pl.when(lane != phase)
+        def _():
+            lend(phase)
 
     for load in loads:
         load.wait()
@@ -390,11 +386,7 @@
         local_kv,
         group_size,
     )
-    project(1, True)
-
-    @pl.when(lane == 1)
-    def _():
-        finish(1)
+    both(1)
 
     for load in late_loads:
         load.wait()
@@ -420,31 +412,29 @@
         local_kv,
         group_size,
     )
-    project(0, False)
-
-    @pl.when(lane == 0)
-    def _():
-        finish(0)
+    both(0)
 
     for peer in peers:
         for copy in kv_copy(me, peer):
             copy.wait_send()
 
-    def drain_parts(c, carry):
+    for c in range(PIECES):
         part_copy(c, 0).wait_send()
-        return carry
-
-    lax.fori_loop(0, PIECES, drain_parts, 0)
-
-    def drain_sends(c, carry):
+    for c in range(SENDS):
         for peer in peers:
             out_copy(c, me, peer).wait_send()
             out_copy(c, peer, peer).wait_recv()
         own_copy(c).wait()
-        return carry
-
-    lax.fori_loop(0, SENDS, drain_sends, 0)
-    hid_copy.wait()
+
+
+def store_kernel(hidden_ref, ffn_ref, hidden_out, ffn_out, sems):
+    copies = [pltpu.make_async_copy(hidden_ref, hidden_out, sems.at[0])]
+    for s in range(ffn_ref.shape[0]):
+        copies.append(pltpu.make_async_copy(ffn_ref.at[s], ffn_out.at[s], sems.at[1 + s]))
+    for copy in copies:
+        copy.start()
+    for copy in copies:
+        copy.wait()
 
 
 def fused_on_device(
@@ -464,13 +454,13 @@
     hidden, arrived = pl.pallas_call(
         functools.partial(fused_kernel, sizes),
         out_shape=(
-            jax.ShapeDtypeStruct((rows, model), bf16),
-            jax.ShapeDtypeStruct((wide_count, capacity, model), bf16),
+            pltpu.VMEM((rows, model), bf16),
+            pltpu.VMEM((wide_count, capacity, model), bf16),
         ),
         in_specs=[pl.BlockSpec(memory_space=pltpu.SMEM), vmem_spec, vmem_spec]
         + [any_spec] * 5
         + [vmem_spec],
-        out_specs=(any_spec, any_spec),
+        out_specs=(vmem_spec, vmem_spec),
         scratch_shapes=[
             pltpu.VMEM(queries.shape, bf16),
             pltpu.VMEM((rows, key_rows.shape[1]), bf16),
@@ -482,7 +472,6 @@
             pltpu.VMEM((2, rows, queries.shape[1]), bf16),
             pltpu.VMEM((2, PIECES, rows, piece), bf16),
             pltpu.VMEM((PIECES, rows, piece), bf16),
-            pltpu.VMEM((rows, model), bf16),
             pltpu.VMEM((SENDS, wide_count, capacity, span), bf16),
             dma((6,)),
             dma((PIECES,)),
@@ -495,22 +484,31 @@
             dma((SENDS, wide_count)),
             dma((SENDS, wide_count)),
             dma((SENDS,)),
-            dma((1,)),
         ],
         compiler_params=pltpu.CompilerParams(
-            collective_id=0, has_side_effects=True, vmem_limit_bytes=56 * 1024 * 1024
+            collective_id=0, has_side_effects=True, vmem_limit_bytes=60 * 1024 * 1024
         ),
     )(
         span_map,
         segments,
-        row_owner,
+        row_owner.reshape(1, rows),
         queries,
         key_rows,
         value_rows,
         residual,
         out_weight,
-        norm_gain.reshape(1, model),
-    )
+        norm_gain.reshape(model // HEAD, HEAD),
+    )
+    hidden, arrived = pl.pallas_call(
+        store_kernel,
+        out_shape=(
+            jax.ShapeDtypeStruct(hidden.shape, bf16),
+            jax.ShapeDtypeStruct(arrived.shape, bf16),
+        ),
+        in_specs=[any_spec] * 2,
+        out_specs=(any_spec, any_spec),
+        scratch_shapes=[dma((1 + wide_count,))],
+    )(hidden, arrived)
     return hidden, arrived.reshape(1, 1, wide_count, capacity, model)
 
 

time: 43 us -> 136 us (3.16)
  Pallas kernels: 35.6 us -> 132 us
  local copies, waits for them, and re-layouts: 6.46 us -> 2.32 us
    pallas_call x1 -> x2, Pallas kernels: 35.6 us -> 132 us  [the longest x1 96.4 us: fused_on_device(): pl.pallas_call(store_kernel, out_shape=(jax.ShapeDtypeStruct(hidden.shape...]
    unnamed x5 -> x4, local copies, waits for them, and re-layouts: 5.15 us -> 2.32 us
where the time goes in v2:
time: 136 us; the launch traced here: 135 us
  Pallas kernels  132 us (97%)
  local copies, waits for them, and re-layouts  2.32 us (2%)
    pallas_call x1, Pallas kernels, fused_on_device(): pl.pallas_call(store_kernel, out_shape=(jax.ShapeDtypeStruct(hidden.shape...  96.4 us
    pallas_call x1, Pallas kernels, fused_on_device(): pl.pallas_call(functools.partial(fused_kernel, sizes), out_shape=(pltpu.V...  36 us

profile of v2, /device:TPU:0, one launch (start us, length us, event | category | flops | bytes accessed | tf_op | source)
XLA Modules:
  0.0 135.5 jit_solution(15510039654390414418)
XLA Ops:
  0.6 36.0 %shard_map.104 = (bf16[128,4096]{1,0:T(8,128)(2,1)S(1)}, bf16[4,64,4096]{2,1,0:T(8,128)(2,1)S(1)}) custom-call(s32[4]{0:T(128)} %span_ref.1, s32[1,128]{1,0:T(1,128)} %seg_ref.1, s32[1,128]{1,0:T(1,128)} %bitcast.4, bf16[256,1024]{1,0:T(8,128)(2,1)} %q_hbm.1, bf16[256,256]{1,0:T(8,128)(2,1)} %k_hbm.1, bf16[256,256]{1,0:T(8,128)(2,1)} %v_hbm.1, ...), custom_call_target="tpu_custom_call" | custom-call | tf_op jit(solution)/shard_map/pallas_call | solution.py:454
  36.7 0.0 copy-start
  36.7 1.3 copy-done
  38.0 0.0 copy-start.1
  38.0 1.0 copy-done.1
  39.0 96.4 %shard_map.105 = (bf16[128,4096]{1,0:T(8,128)(2,1)}, bf16[4,64,4096]{2,1,0:T(8,128)(2,1)}) custom-call(bf16[128,4096]{1,0:T(8,128)(2,1)} %copy-done.1, bf16[4,64,4096]{2,1,0:T(8,128)(2,1)} %copy-done), custom_call_target="tpu_custom_call" | custom-call | tf_op jit(solution)/shard_map/pallas_call | solution.py:502
Async XLA Ops:
  36.7 1.3 copy-start
  38.0 1.0 copy-start.1

commit v3 on v2

--- a/solution.py
+++ b/solution.py
@@ -173,12 +173,16 @@
     score_scale = HEAD ** (-0.5)
     count = rows.stop - rows.start
     tiled = jnp.concatenate([visible] * group_size, axis=0)
-    for g in range(local_kv):
-        heads = [g * group_size + j for j in range(group_size)]
-        stacked = jnp.concatenate([q_buf[rows, h * HEAD : (h + 1) * HEAD] for h in heads], axis=0)
+
+    def attend_group(g, carry):
+        heads = [
+            pl.ds(pl.multiple_of((g * group_size + j) * HEAD, HEAD), HEAD) for j in range(group_size)
+        ]
+        group = pl.ds(pl.multiple_of(g * HEAD, HEAD), HEAD)
+        stacked = jnp.concatenate([q_buf[rows, h] for h in heads], axis=0)
         scores = (
             lax.dot_general(
-                stacked, keys(g), (((1,), (1,)), ((), ())), preferred_element_type=jnp.float32
+                stacked, keys(group), (((1,), (1,)), ((), ())), preferred_element_type=jnp.float32
             )
             * score_scale
         )
@@ -186,11 +190,14 @@
         weights = jnp.exp(masked - jnp.max(masked, axis=1, keepdims=True))
         total = jnp.sum(weights, axis=1, keepdims=True)
         mixed = jnp.dot(
-            weights.astype(jnp.bfloat16), values(g), preferred_element_type=jnp.float32
+            weights.astype(jnp.bfloat16), values(group), preferred_element_type=jnp.float32
         )
         mixed = (mixed / total).astype(jnp.bfloat16)
         for j, h in enumerate(heads):
-            out_buf[lane, :, h * HEAD : (h + 1) * HEAD] = mixed[j * count : (j + 1) * count]
+            out_buf[lane, :, h] = mixed[j * count : (j + 1) * count]
+        return carry
+
+    lax.fori_loop(0, local_kv, attend_group, 0)
 
 
 def fused_kernel(
@@ -217,6 +224,7 @@
     part_buf,
     recv_buf,
     out_buf,
+    gain_buf,
     in_sem,
     w_sem,
     k_send,
@@ -307,19 +315,26 @@
 
     def project(phase, c):
         if phase == 1:
-            w_loads[c].wait()
+            pltpu.make_async_copy(
+                w_hbm.at[:, pl.ds(pl.multiple_of(c * piece, piece), piece)],
+                w_buf.at[c],
+                w_sem.at[c],
+            ).wait()
         product = jnp.dot(att_buf[phase], w_buf[c], preferred_element_type=jnp.float32)
         part_buf[phase, c] = product.astype(jnp.bfloat16)
 
     def lend(phase):
-        for c in range(PIECES):
+        def step(c, carry):
             project(phase, c)
             part_copy(c, phase).start()
+            return carry
+
+        lax.fori_loop(0, PIECES, step, 0)
 
     def out_copy(c, source, peer):
         return pltpu.make_async_remote_copy(
             src_ref=out_buf.at[c, peer],
-            dst_ref=ffn_ref.at[source, :, pl.ds(c * span, span)],
+            dst_ref=ffn_ref.at[source, :, pl.ds(pl.multiple_of(c * span, span), span)],
             send_sem=o_send.at[c, peer],
             recv_sem=o_recv.at[c, source],
             device_id={"wide": peer},
@@ -329,31 +344,36 @@
     def own_copy(c):
         return pltpu.make_async_copy(
             out_buf.at[c, me],
-            ffn_ref.at[me, :, pl.ds(c * span, span)],
+            ffn_ref.at[me, :, pl.ds(pl.multiple_of(c * span, span), span)],
             own_sem.at[c],
         )
 
     def finish(phase):
         res_load.wait()
-        squares = jnp.zeros((rows, 1), jnp.float32)
-        for step in range(PIECES + 1):
-            if step < PIECES:
-                project(phase, step)
-            if step == 0:
-                continue
-            c = step - 1
+
+        def add_piece(c, squares):
             part_copy(c, phase).wait_recv()
-            cols = slice(c * piece, (c + 1) * piece)
+            cols = pl.ds(pl.multiple_of(c * piece, piece), piece)
             summed = part_buf[phase, c].astype(jnp.float32) + recv_buf[c].astype(jnp.float32)
             hidden = (res_buf[:, cols].astype(jnp.float32) + summed).astype(jnp.bfloat16)
             hidden_ref[:, cols] = hidden
             widened = hidden.astype(jnp.float32)
-            squares += jnp.sum(widened * widened, axis=1, keepdims=True)
+            return squares + jnp.sum(widened * widened, axis=1, keepdims=True)
+
+        def step(c, squares):
+            project(phase, c)
+            return add_piece(c - 1, squares)
+
+        project(phase, 0)
+        squares = lax.fori_loop(1, PIECES, step, jnp.zeros((rows, 1), jnp.float32))
+        squares = add_piece(PIECES - 1, squares)
         factor = lax.rsqrt(squares / model + 1e-05)
         lines = span // HEAD
-        for c in range(SENDS):
-            cols = slice(c * span, (c + 1) * span)
-            gains = gain_ref[c * lines : (c + 1) * lines, :].astype(jnp.float32)
+        gain_buf[...] = gain_ref[...].astype(jnp.float32)
+
+        def send_piece(c, carry):
+            cols = pl.ds(pl.multiple_of(c * span, span), span)
+            gains = gain_buf[pl.ds(pl.multiple_of(c * lines, lines), lines), :]
             gain = jnp.concatenate([gains[i : i + 1] for i in range(lines)], axis=1)
             normed = (hidden_ref[:, cols].astype(jnp.float32) * factor * gain).astype(jnp.bfloat16)
             outgoing = jnp.dot(dispatch, normed, preferred_element_type=jnp.float32)
@@ -361,6 +381,9 @@
             for peer in peers:
                 out_copy(c, me, peer).start()
             own_copy(c).start()
+            return carry
+
+        lax.fori_loop(0, SENDS, send_piece, 0)
 
     def both(phase):
         @pl.when(lane == phase)
@@ -377,8 +400,8 @@
     short_visible = (seg_across == seg_across.T) & (col_id <= row_id)
     attend_heads(
         q_buf,
-        lambda g: ks_buf[:, g * HEAD : (g + 1) * HEAD],
-        lambda g: vs_buf[:, g * HEAD : (g + 1) * HEAD],
+        lambda group: ks_buf[:, group],
+        lambda group: vs_buf[:, group],
         short_visible,
         short_rows,
         att_buf,
@@ -403,8 +426,8 @@
     )
     attend_heads(
         q_buf,
-        lambda g: k_buf[:, :, g * HEAD : (g + 1) * HEAD].reshape(wide_count * rows, HEAD),
-        lambda g: v_buf[:, :, g * HEAD : (g + 1) * HEAD].reshape(wide_count * rows, HEAD),
+        lambda group: k_buf[:, :, group].reshape(wide_count * rows, HEAD),
+        lambda group: v_buf[:, :, group].reshape(wide_count * rows, HEAD),
         long_visible,
         long_rows,
         att_buf,
@@ -418,13 +441,20 @@
         for copy in kv_copy(me, peer):
             copy.wait_send()
 
-    for c in range(PIECES):
+    def drain_parts(c, carry):
         part_copy(c, 0).wait_send()
-    for c in range(SENDS):
+        return carry
+
+    lax.fori_loop(0, PIECES, drain_parts, 0)
+
+    def drain_sends(c, carry):
         for peer in peers:
             out_copy(c, me, peer).wait_send()
             out_copy(c, peer, peer).wait_recv()
         own_copy(c).wait()
+        return carry
+
+    lax.fori_loop(0, SENDS, drain_sends, 0)
 
 
 def store_kernel(hidden_ref, ffn_ref, hidden_out, ffn_out, sems):
@@ -473,6 +503,7 @@
             pltpu.VMEM((2, PIECES, rows, piece), bf16),
             pltpu.VMEM((PIECES, rows, piece), bf16),
             pltpu.VMEM((SENDS, wide_count, capacity, span), bf16),
+            pltpu.VMEM((model // HEAD, HEAD), jnp.float32),
             dma((6,)),
             dma((PIECES,)),
             dma((wide_count,)),
@@ -508,6 +539,7 @@
         in_specs=[any_spec] * 2,
         out_specs=(any_spec, any_spec),
         scratch_shapes=[dma((1 + wide_count,))],
+        compiler_params=pltpu.CompilerParams(vmem_limit_bytes=1024 * 1024),
     )(hidden, arrived)
     return hidden, arrived.reshape(1, 1, wide_count, capacity, model)
 

time: 136 us -> 38.9 us (0.29)
  Pallas kernels: 132 us -> 38.1 us
  local copies, waits for them, and re-layouts: 2.32 us -> 0 us
    pallas_call x1, Pallas kernels: 96.4 us -> 1.7 us  [fused_on_device(): pl.pallas_call(store_kernel, out_shape=(jax.ShapeDtypeStruct(hidden.shape...]
    unnamed x4 -> x0, local copies, waits for them, and re-layouts: 2.32 us -> none
where the time goes in v3:
time: 38.9 us; the launch traced here: 38.7 us
  Pallas kernels  38.1 us (98%)
  between operations  0.64 us (2%)
    pallas_call x1, Pallas kernels, fused_on_device(): pl.pallas_call(functools.partial(fused_kernel, sizes), out_shape=(pltpu.V...  36.4 us
    pallas_call x1, Pallas kernels, fused_on_device(): pl.pallas_call(store_kernel, out_shape=(jax.ShapeDtypeStruct(hidden.shape...  1.7 us

profile of v3, /device:TPU:0, one launch (start us, length us, event | category | flops | bytes accessed | tf_op | source)
XLA Modules:
  0.0 38.7 jit_solution(12435541697486537562)
XLA Ops:
  0.6 36.4 %shard_map.104 = (bf16[128,4096]{1,0:T(8,128)(2,1)S(1)}, bf16[4,64,4096]{2,1,0:T(8,128)(2,1)S(1)}) custom-call(s32[4]{0:T(128)} %span_ref.1, s32[1,128]{1,0:T(1,128)} %seg_ref.1, s32[1,128]{1,0:T(1,128)} %bitcast.4, bf16[256,1024]{1,0:T(8,128)(2,1)} %q_hbm.1, bf16[256,256]{1,0:T(8,128)(2,1)} %k_hbm.1, bf16[256,256]{1,0:T(8,128)(2,1)} %v_hbm.1, ...), custom_call_target="tpu_custom_call" | custom-call | tf_op jit(solution)/shard_map/pallas_call | solution.py:484
  37.0 1.7 %shard_map.105 = (bf16[128,4096]{1,0:T(8,128)(2,1)}, bf16[4,64,4096]{2,1,0:T(8,128)(2,1)}) custom-call(bf16[128,4096]{1,0:T(8,128)(2,1)S(1)} %get-tuple-element.6.hidden_ref, bf16[4,64,4096]{2,1,0:T(8,128)(2,1)S(1)} %get-tuple-element.7.ffn_ref), custom_call_target="tpu_custom_call" | custom-call | tf_op jit(solution)/shard_map/pallas_call | solution.py:533

commit v4 on v3

--- a/solution.py
+++ b/solution.py
@@ -224,13 +224,12 @@
     part_buf,
     recv_buf,
     out_buf,
+    relay_buf,
     gain_buf,
     in_sem,
     w_sem,
-    k_send,
-    k_recv,
-    v_send,
-    v_recv,
+    kv_send,
+    kv_recv,
     p_send,
     p_recv,
     o_send,
@@ -244,7 +243,10 @@
     me = lax.axis_index("wide")
     lane = lax.axis_index("narrow")
     other = 1 - lane
-    peers = [lax.rem(me + k, wide_count) for k in range(1, wide_count)]
+    half = capacity // 2
+    along, across = lax.rem(me, 2), me // 2
+    near = [across * 2 + 1 - along, (1 - across) * 2 + along]
+    far = (1 - across) * 2 + 1 - along
     long_rows, short_rows = slice(0, rows), slice(rows, 2 * rows)
 
     loads = [
@@ -267,30 +269,23 @@
         load.start()
 
     barrier = pltpu.get_barrier_semaphore()
-    for peer in peers:
+    for peer in near:
         pl.semaphore_signal(barrier, inc=1, device_id={"wide": peer}, device_id_type=MESH)
     pl.semaphore_signal(barrier, inc=1, device_id={"narrow": other}, device_id_type=MESH)
-    pl.semaphore_wait(barrier, wide_count)
-
-    def kv_copy(source, peer):
-        return [
-            pltpu.make_async_remote_copy(
-                src_ref=hbm.at[pl.ds(0, rows)],
-                dst_ref=buf.at[source],
-                send_sem=send.at[peer],
-                recv_sem=recv.at[source],
-                device_id={"wide": peer},
-                device_id_type=MESH,
-            )
-            for hbm, buf, send, recv in (
-                (k_hbm, k_buf, k_send, k_recv),
-                (v_hbm, v_buf, v_send, v_recv),
-            )
-        ]
-
-    for peer in peers:
-        for copy in kv_copy(me, peer):
-            copy.start()
+
+    def kv_copy(i, source, peer, first, sem):
+        hbm, buf = ((k_hbm, k_buf), (v_hbm, v_buf))[i]
+        return pltpu.make_async_remote_copy(
+            src_ref=hbm.at[pl.ds(0, rows)] if first else buf.at[source],
+            dst_ref=buf.at[source],
+            send_sem=kv_send.at[i, sem],
+            recv_sem=kv_recv.at[i, source],
+            device_id={"wide": peer},
+            device_id_type=MESH,
+        )
+
+    kv_first = [kv_copy(i, me, near[j], True, j) for i in range(2) for j in range(2)]
+    kv_forward = [kv_copy(i, near[i], near[1 - i], False, 2) for i in range(2)]
 
     row_id = lax.broadcasted_iota(jnp.int32, (rows, rows), 0)
     col_id = lax.broadcasted_iota(jnp.int32, (rows, rows), 1)
@@ -302,6 +297,10 @@
     target = (owner_across[0:1] * capacity + slot).astype(jnp.int32)
     slots = lax.broadcasted_iota(jnp.int32, (wide_count * capacity, rows), 0)
     dispatch = jnp.where(slots == target, 1.0, 0.0).astype(jnp.bfloat16)
+
+    pl.semaphore_wait(barrier, 3)
+    for copy in kv_first:
+        copy.start()
 
     def part_copy(c, phase):
         return pltpu.make_async_remote_copy(
@@ -323,6 +322,10 @@
         product = jnp.dot(att_buf[phase], w_buf[c], preferred_element_type=jnp.float32)
         part_buf[phase, c] = product.astype(jnp.bfloat16)
 
+    def send_values_on():
+        kv_copy(1, near[1], near[1], True, 1).wait_recv()
+        kv_forward[1].start()
+
     def lend(phase):
         def step(c, carry):
             project(phase, c)
@@ -330,14 +333,37 @@
             return carry
 
         lax.fori_loop(0, PIECES, step, 0)
-
-    def out_copy(c, source, peer):
+        if phase == 1:
+            send_values_on()
+
+    def direct_copy(c, j, source):
         return pltpu.make_async_remote_copy(
-            src_ref=out_buf.at[c, peer],
+            src_ref=out_buf.at[c, near[j]],
             dst_ref=ffn_ref.at[source, :, pl.ds(pl.multiple_of(c * span, span), span)],
-            send_sem=o_send.at[c, peer],
-            recv_sem=o_recv.at[c, source],
-            device_id={"wide": peer},
+            send_sem=o_send.at[c, j],
+            recv_sem=o_recv.at[c, j],
+            device_id={"wide": near[j]},
+            device_id_type=MESH,
+        )
+
+    def relay_copy(c, j):
+        return pltpu.make_async_remote_copy(
+            src_ref=out_buf.at[c, far, pl.ds(j * half, half)],
+            dst_ref=relay_buf.at[c, j],
+            send_sem=o_send.at[c, 2 + j],
+            recv_sem=o_recv.at[c, 2 + j],
+            device_id={"wide": near[j]},
+            device_id_type=MESH,
+        )
+
+    def forward_copy(c, j, source):
+        cols = pl.ds(pl.multiple_of(c * span, span), span)
+        return pltpu.make_async_remote_copy(
+            src_ref=relay_buf.at[c, j],
+            dst_ref=ffn_ref.at[source, pl.ds(j * half, half), cols],
+            send_sem=o_send.at[c, 4 + j],
+            recv_sem=o_recv.at[c, 4 + j],
+            device_id={"wide": near[1 - j]},
             device_id_type=MESH,
         )
 
@@ -366,6 +392,8 @@
 
         project(phase, 0)
         squares = lax.fori_loop(1, PIECES, step, jnp.zeros((rows, 1), jnp.float32))
+        if phase == 1:
+            send_values_on()
         squares = add_piece(PIECES - 1, squares)
         factor = lax.rsqrt(squares / model + 1e-05)
         lines = span // HEAD
@@ -378,8 +406,10 @@
             normed = (hidden_ref[:, cols].astype(jnp.float32) * factor * gain).astype(jnp.bfloat16)
             outgoing = jnp.dot(dispatch, normed, preferred_element_type=jnp.float32)
             out_buf[c] = outgoing.astype(jnp.bfloat16).reshape(wide_count, capacity, span)
-            for peer in peers:
-                out_copy(c, me, peer).start()
+            for j in range(2):
+                relay_copy(c, j).start()
+            for j in range(2):
+                direct_copy(c, j, me).start()
             own_copy(c).start()
             return carry
 
@@ -409,13 +439,16 @@
         local_kv,
         group_size,
     )
+    kv_copy(0, near[0], near[0], True, 0).wait_recv()
+    kv_forward[0].start()
     both(1)
 
     for load in late_loads:
         load.wait()
-    for peer in peers:
-        for copy in kv_copy(peer, peer):
-            copy.wait_recv()
+    kv_copy(0, near[1], near[1], True, 1).wait_recv()
+    kv_copy(1, near[0], near[0], True, 0).wait_recv()
+    for i in range(2):
+        kv_copy(i, far, near[1 - i], False, 2).wait_recv()
     own_span = span_ref[me]
     long_visible = jnp.concatenate(
         [
@@ -437,9 +470,16 @@
     )
     both(0)
 
-    for peer in peers:
-        for copy in kv_copy(me, peer):
-            copy.wait_send()
+    def forward(c, carry):
+        for j in range(2):
+            relay_copy(c, j).wait_recv()
+            forward_copy(c, j, near[j]).start()
+        return carry
+
+    lax.fori_loop(0, SENDS, forward, 0)
+
+    for copy in kv_first + kv_forward:
+        copy.wait_send()
 
     def drain_parts(c, carry):
         part_copy(c, 0).wait_send()
@@ -448,9 +488,12 @@
     lax.fori_loop(0, PIECES, drain_parts, 0)
 
     def drain_sends(c, carry):
-        for peer in peers:
-            out_copy(c, me, peer).wait_send()
-            out_copy(c, peer, peer).wait_recv()
+        for j in range(2):
+            relay_copy(c, j).wait_send()
+            direct_copy(c, j, me).wait_send()
+            direct_copy(c, j, near[j]).wait_recv()
+            forward_copy(c, j, near[j]).wait_send()
+            forward_copy(c, j, far).wait_recv()
         own_copy(c).wait()
         return carry
 
@@ -503,17 +546,16 @@
             pltpu.VMEM((2, PIECES, rows, piece), bf16),
             pltpu.VMEM((PIECES, rows, piece), bf16),
             pltpu.VMEM((SENDS, wide_count, capacity, span), bf16),
+            pltpu.VMEM((SENDS, 2, capacity // 2, span), bf16),
             pltpu.VMEM((model // HEAD, HEAD), jnp.float32),
             dma((6,)),
             dma((PIECES,)),
-            dma((wide_count,)),
-            dma((wide_count,)),
-            dma((wide_count,)),
-            dma((wide_count,)),
+            dma((2, 3)),
+            dma((2, wide_count)),
             dma((PIECES,)),
             dma((PIECES,)),
-            dma((SENDS, wide_count)),
-            dma((SENDS, wide_count)),
+            dma((SENDS, 6)),
+            dma((SENDS, 6)),
             dma((SENDS,)),
         ],
         compiler_params=pltpu.CompilerParams(
@@ -552,7 +594,8 @@
         lax.axis_size("narrow") == 2
         and rows == LONG_DEV
         and queries.shape[0] == 2 * LONG_DEV
-        and (2 * rows) % (16 * wide_count) == 0
+        and wide_count == 4
+        and (2 * rows) % (32 * wide_count) == 0
         and model % (PIECES * HEAD) == 0
     )
     return (fused_on_device if fits else general_on_device)(*args)

time: 38.9 us -> 40.7 us (1.046)
  Pallas kernels: 38.1 us -> 39.9 us
    pallas_call x1, Pallas kernels: 36.4 us -> 38.2 us  [fused_on_device(): pl.pallas_call(functools.partial(fused_kernel, sizes), out_shape=(pltpu.V...]
where the time goes in v4:
time: 40.7 us; the launch traced here: 40.5 us
  Pallas kernels  39.9 us (98%)
  between operations  0.64 us (2%)
    pallas_call x1, Pallas kernels, fused_on_device(): pl.pallas_call(functools.partial(fused_kernel, sizes), out_shape=(pltpu.V...  38.2 us
    pallas_call x1, Pallas kernels, fused_on_device(): pl.pallas_call(store_kernel, out_shape=(jax.ShapeDtypeStruct(hidden.shape...  1.7 us

profile of v4, /device:TPU:0, one launch (start us, length us, event | category | flops | bytes accessed | tf_op | source)
XLA Modules:
  0.0 40.5 jit_solution(14182424873343301835)
XLA Ops:
  0.6 38.2 %shard_map.104 = (bf16[128,4096]{1,0:T(8,128)(2,1)S(1)}, bf16[4,64,4096]{2,1,0:T(8,128)(2,1)S(1)}) custom-call(s32[4]{0:T(128)} %span_ref.1, s32[1,128]{1,0:T(1,128)} %seg_ref.1, s32[1,128]{1,0:T(1,128)} %bitcast.4, bf16[256,1024]{1,0:T(8,128)(2,1)} %q_hbm.1, bf16[256,256]{1,0:T(8,128)(2,1)} %k_hbm.1, bf16[256,256]{1,0:T(8,128)(2,1)} %v_hbm.1, ...), custom_call_target="tpu_custom_call" | custom-call | tf_op jit(solution)/shard_map/pallas_call | solution.py:527
  38.8 1.7 %shard_map.105 = (bf16[128,4096]{1,0:T(8,128)(2,1)}, bf16[4,64,4096]{2,1,0:T(8,128)(2,1)}) custom-call(bf16[128,4096]{1,0:T(8,128)(2,1)S(1)} %get-tuple-element.6.hidden_ref, bf16[4,64,4096]{2,1,0:T(8,128)(2,1)S(1)} %get-tuple-element.7.ffn_ref), custom_call_target="tpu_custom_call" | custom-call | tf_op jit(solution)/shard_map/pallas_call | solution.py:575

commit v5 on v2

--- a/solution.py
+++ b/solution.py
@@ -173,12 +173,16 @@
     score_scale = HEAD ** (-0.5)
     count = rows.stop - rows.start
     tiled = jnp.concatenate([visible] * group_size, axis=0)
-    for g in range(local_kv):
-        heads = [g * group_size + j for j in range(group_size)]
-        stacked = jnp.concatenate([q_buf[rows, h * HEAD : (h + 1) * HEAD] for h in heads], axis=0)
+
+    def attend_group(g, carry):
+        heads = [
+            pl.ds(pl.multiple_of((g * group_size + j) * HEAD, HEAD), HEAD) for j in range(group_size)
+        ]
+        group = pl.ds(pl.multiple_of(g * HEAD, HEAD), HEAD)
+        stacked = jnp.concatenate([q_buf[rows, h] for h in heads], axis=0)
         scores = (
             lax.dot_general(
-                stacked, keys(g), (((1,), (1,)), ((), ())), preferred_element_type=jnp.float32
+                stacked, keys(group), (((1,), (1,)), ((), ())), preferred_element_type=jnp.float32
             )
             * score_scale
         )
@@ -186,24 +190,27 @@
         weights = jnp.exp(masked - jnp.max(masked, axis=1, keepdims=True))
         total = jnp.sum(weights, axis=1, keepdims=True)
         mixed = jnp.dot(
-            weights.astype(jnp.bfloat16), values(g), preferred_element_type=jnp.float32
+            weights.astype(jnp.bfloat16), values(group), preferred_element_type=jnp.float32
         )
         mixed = (mixed / total).astype(jnp.bfloat16)
         for j, h in enumerate(heads):
-            out_buf[lane, :, h * HEAD : (h + 1) * HEAD] = mixed[j * count : (j + 1) * count]
+            out_buf[lane, :, h] = mixed[j * count : (j + 1) * count]
+        return carry
+
+    lax.fori_loop(0, local_kv, attend_group, 0)
 
 
 def fused_kernel(
     sizes,
-    span_ref,
-    seg_ref,
-    owner_ref,
+    span_hbm,
+    seg_hbm,
+    owner_hbm,
     q_hbm,
     k_hbm,
     v_hbm,
     res_hbm,
     w_hbm,
-    gain_ref,
+    gain_hbm,
     hidden_ref,
     ffn_ref,
     q_buf,
@@ -217,6 +224,10 @@
     part_buf,
     recv_buf,
     out_buf,
+    gain_ref,
+    span_ref,
+    seg_ref,
+    owner_ref,
     in_sem,
     w_sem,
     k_send,
@@ -239,14 +250,24 @@
     peers = [lax.rem(me + k, wide_count) for k in range(1, wide_count)]
     long_rows, short_rows = slice(0, rows), slice(rows, 2 * rows)
 
+    barrier = pltpu.get_barrier_semaphore()
+    for peer in peers:
+        pl.semaphore_signal(barrier, inc=1, device_id={"wide": peer}, device_id_type=MESH)
+    pl.semaphore_signal(barrier, inc=1, device_id={"narrow": other}, device_id_type=MESH)
+
     loads = [
-        pltpu.make_async_copy(q_hbm, q_buf, in_sem.at[0]),
+        pltpu.make_async_copy(q_hbm.at[pl.ds(rows, rows)], q_buf.at[pl.ds(rows, rows)], in_sem.at[0]),
         pltpu.make_async_copy(k_hbm.at[pl.ds(rows, rows)], ks_buf, in_sem.at[1]),
         pltpu.make_async_copy(v_hbm.at[pl.ds(rows, rows)], vs_buf, in_sem.at[2]),
+        pltpu.make_async_copy(seg_hbm, seg_ref, in_sem.at[6]),
     ]
+    owner_load = pltpu.make_async_copy(owner_hbm, owner_ref, in_sem.at[7])
+    gain_load = pltpu.make_async_copy(gain_hbm, gain_ref, in_sem.at[9])
     late_loads = [
         pltpu.make_async_copy(k_hbm.at[pl.ds(0, rows)], k_buf.at[me], in_sem.at[3]),
         pltpu.make_async_copy(v_hbm.at[pl.ds(0, rows)], v_buf.at[me], in_sem.at[4]),
+        pltpu.make_async_copy(span_hbm, span_ref, in_sem.at[8]),
+        pltpu.make_async_copy(q_hbm.at[pl.ds(0, rows)], q_buf.at[pl.ds(0, rows)], in_sem.at[10]),
     ]
     res_load = pltpu.make_async_copy(res_hbm, res_buf, in_sem.at[5])
     w_loads = [
@@ -255,13 +276,9 @@
         )
         for c in range(PIECES)
     ]
-    for load in loads + w_loads + [res_load] + late_loads:
+    for load in loads + [owner_load] + w_loads + [res_load, gain_load] + late_loads:
         load.start()
 
-    barrier = pltpu.get_barrier_semaphore()
-    for peer in peers:
-        pl.semaphore_signal(barrier, inc=1, device_id={"wide": peer}, device_id_type=MESH)
-    pl.semaphore_signal(barrier, inc=1, device_id={"narrow": other}, device_id_type=MESH)
     pl.semaphore_wait(barrier, wide_count)
 
     def kv_copy(source, peer):
@@ -287,6 +304,7 @@
     row_id = lax.broadcasted_iota(jnp.int32, (rows, rows), 0)
     col_id = lax.broadcasted_iota(jnp.int32, (rows, rows), 1)
 
+    owner_load.wait()
     owner_across = jnp.broadcast_to(owner_ref[...], (rows, rows)).astype(jnp.float32)
     owner_down = owner_across.T
     same = jnp.where((owner_down == owner_across) & (row_id < col_id), 1.0, 0.0)
@@ -319,7 +337,7 @@
     def out_copy(c, source, peer):
         return pltpu.make_async_remote_copy(
             src_ref=out_buf.at[c, peer],
-            dst_ref=ffn_ref.at[source, :, pl.ds(c * span, span)],
+            dst_ref=ffn_ref.at[source, :, pl.ds(pl.multiple_of(c * span, span), span)],
             send_sem=o_send.at[c, peer],
             recv_sem=o_recv.at[c, source],
             device_id={"wide": peer},
@@ -329,12 +347,13 @@
     def own_copy(c):
         return pltpu.make_async_copy(
             out_buf.at[c, me],
-            ffn_ref.at[me, :, pl.ds(c * span, span)],
+            ffn_ref.at[me, :, pl.ds(pl.multiple_of(c * span, span), span)],
             own_sem.at[c],
         )
 
     def finish(phase):
         res_load.wait()
+        gain_load.wait()
         squares = jnp.zeros((rows, 1), jnp.float32)
         for step in range(PIECES + 1):
             if step < PIECES:
@@ -377,8 +396,8 @@
     short_visible = (seg_across == seg_across.T) & (col_id <= row_id)
     attend_heads(
         q_buf,
-        lambda g: ks_buf[:, g * HEAD : (g + 1) * HEAD],
-        lambda g: vs_buf[:, g * HEAD : (g + 1) * HEAD],
+        lambda group: ks_buf[:, group],
+        lambda group: vs_buf[:, group],
         short_visible,
         short_rows,
         att_buf,
@@ -393,18 +412,20 @@
     for peer in peers:
         for copy in kv_copy(peer, peer):
             copy.wait_recv()
-    own_span = span_ref[me]
+    spans = span_ref[...]
+    wide_ids = lax.broadcasted_iota(jnp.int32, (1, wide_count), 1)
+    own_span = jnp.sum(jnp.where(wide_ids == me, spans, 0), axis=1, keepdims=True)
     long_visible = jnp.concatenate(
         [
-            (span_ref[b] * rows + col_id) <= (own_span * rows + row_id)
+            (spans[:, b : b + 1] * rows + col_id) <= (own_span * rows + row_id)
             for b in range(wide_count)
         ],
         axis=1,
     )
     attend_heads(
         q_buf,
-        lambda g: k_buf[:, :, g * HEAD : (g + 1) * HEAD].reshape(wide_count * rows, HEAD),
-        lambda g: v_buf[:, :, g * HEAD : (g + 1) * HEAD].reshape(wide_count * rows, HEAD),
+        lambda group: k_buf[:, :, group].reshape(wide_count * rows, HEAD),
+        lambda group: v_buf[:, :, group].reshape(wide_count * rows, HEAD),
         long_visible,
         long_rows,
         att_buf,
@@ -418,19 +439,39 @@
         for copy in kv_copy(me, peer):
             copy.wait_send()
 
-    for c in range(PIECES):
+    def drain_parts(c, carry):
         part_copy(c, 0).wait_send()
-    for c in range(SENDS):
+        return carry
+
+    lax.fori_loop(0, PIECES, drain_parts, 0)
+
+    def drain_sends(c, carry):
         for peer in peers:
             out_copy(c, me, peer).wait_send()
             out_copy(c, peer, peer).wait_recv()
         own_copy(c).wait()
+        return carry
+
+    lax.fori_loop(0, SENDS, drain_sends, 0)
 
 
 def store_kernel(hidden_ref, ffn_ref, hidden_out, ffn_out, sems):
-    copies = [pltpu.make_async_copy(hidden_ref, hidden_out, sems.at[0])]
-    for s in range(ffn_ref.shape[0]):
-        copies.append(pltpu.make_async_copy(ffn_ref.at[s], ffn_out.at[s], sems.at[1 + s]))
+    parts = ffn_ref.shape[0]
+    count = hidden_ref.shape[0] // parts
+    half = ffn_ref.shape[1] // 2
+    copies = []
+    for s in range(parts):
+        some = pl.ds(s * count, count)
+        copies.append(
+            pltpu.make_async_copy(hidden_ref.at[some], hidden_out.at[some], sems.at[3 * s])
+        )
+        for j in range(2):
+            some = pl.ds(j * half, half)
+            copies.append(
+                pltpu.make_async_copy(
+                    ffn_ref.at[s, some], ffn_out.at[s, some], sems.at[3 * s + 1 + j]
+                )
+            )
     for copy in copies:
         copy.start()
     for copy in copies:
@@ -457,9 +498,7 @@
             pltpu.VMEM((rows, model), bf16),
             pltpu.VMEM((wide_count, capacity, model), bf16),
         ),
-        in_specs=[pl.BlockSpec(memory_space=pltpu.SMEM), vmem_spec, vmem_spec]
-        + [any_spec] * 5
-        + [vmem_spec],
+        in_specs=[any_spec] * 9,
         out_specs=(vmem_spec, vmem_spec),
         scratch_shapes=[
             pltpu.VMEM(queries.shape, bf16),
@@ -473,7 +512,11 @@
             pltpu.VMEM((2, PIECES, rows, piece), bf16),
             pltpu.VMEM((PIECES, rows, piece), bf16),
             pltpu.VMEM((SENDS, wide_count, capacity, span), bf16),
-            dma((6,)),
+            pltpu.VMEM((model // HEAD, HEAD), bf16),
+            pltpu.VMEM((1, wide_count), jnp.int32),
+            pltpu.VMEM((1, rows), jnp.int32),
+            pltpu.VMEM((1, rows), jnp.int32),
+            dma((11,)),
             dma((PIECES,)),
             dma((wide_count,)),
             dma((wide_count,)),
@@ -489,7 +532,7 @@
             collective_id=0, has_side_effects=True, vmem_limit_bytes=60 * 1024 * 1024
         ),
     )(
-        span_map,
+        span_map.reshape(1, wide_count),
         segments,
         row_owner.reshape(1, rows),
         queries,
@@ -507,7 +550,8 @@
         ),
         in_specs=[any_spec] * 2,
         out_specs=(any_spec, any_spec),
-        scratch_shapes=[dma((1 + wide_count,))],
+        scratch_shapes=[dma((3 * wide_count,))],
+        compiler_params=pltpu.CompilerParams(vmem_limit_bytes=1024 * 1024),
     )(hidden, arrived)
     return hidden, arrived.reshape(1, 1, wide_count, capacity, model)
 
@@ -520,7 +564,8 @@
         lax.axis_size("narrow") == 2
         and rows == LONG_DEV
         and queries.shape[0] == 2 * LONG_DEV
-        and (2 * rows) % (16 * wide_count) == 0
+        and (2 * rows) % (32 * wide_count) == 0
+        and rows % (16 * wide_count) == 0
         and model % (PIECES * HEAD) == 0
     )
     return (fused_on_device if fits else general_on_device)(*args)

time: 136 us -> 37.5 us (0.28)
  Pallas kernels: 132 us -> 36.7 us
  local copies, waits for them, and re-layouts: 2.32 us -> 0 us
    pallas_call x1, Pallas kernels: 96.4 us -> 1.76 us  [fused_on_device(): pl.pallas_call(store_kernel, out_shape=(jax.ShapeDtypeStruct(hidden.shape...]
    unnamed x4 -> x0, local copies, waits for them, and re-layouts: 2.32 us -> none
where the time goes in v5:
time: 37.5 us; the launch traced here: 37.3 us
  Pallas kernels  36.7 us (98%)
  between operations  0.64 us (2%)
    pallas_call x1, Pallas kernels, fused_on_device(): pl.pallas_call(functools.partial(fused_kernel, sizes), out_shape=(pltpu.V...  34.9 us
    pallas_call x1, Pallas kernels, fused_on_device(): pl.pallas_call(store_kernel, out_shape=(jax.ShapeDtypeStruct(hidden.shape...  1.76 us

profile of v5, /device:TPU:0, one launch (start us, length us, event | category | flops | bytes accessed | tf_op | source)
XLA Modules:
  0.0 37.3 jit_solution(7674597541489050967)
XLA Ops:
  0.6 34.9 %shard_map.104 = (bf16[128,4096]{1,0:T(8,128)(2,1)S(1)}, bf16[4,64,4096]{2,1,0:T(8,128)(2,1)S(1)}) custom-call(s32[1,4]{1,0:T(1,128)} %bitcast.5, s32[1,128]{1,0:T(1,128)} %seg_hbm.1, s32[1,128]{1,0:T(1,128)} %bitcast.6, bf16[256,1024]{1,0:T(8,128)(2,1)} %q_hbm.1, bf16[256,256]{1,0:T(8,128)(2,1)} %k_hbm.1, bf16[256,256]{1,0:T(8,128)(2,1)} %v_hbm.1, ...), custom_call_target="tpu_custom_call" | custom-call | tf_op jit(solution)/shard_map/pallas_call | solution.py:495
  35.5 1.8 %shard_map.105 = (bf16[128,4096]{1,0:T(8,128)(2,1)}, bf16[4,64,4096]{2,1,0:T(8,128)(2,1)}) custom-call(bf16[128,4096]{1,0:T(8,128)(2,1)S(1)} %get-tuple-element.6.hidden_ref, bf16[4,64,4096]{2,1,0:T(8,128)(2,1)S(1)} %get-tuple-element.7.ffn_ref), custom_call_target="tpu_custom_call" | custom-call | tf_op jit(solution)/shard_map/pallas_call | solution.py:545

commit v6 on v5

--- a/solution.py
+++ b/solution.py
@@ -169,7 +169,7 @@
 MESH = pl.DeviceIdType.MESH
 
 
-def attend_heads(q_buf, keys, values, visible, rows, out_buf, lane, local_kv, group_size):
+def attend_heads(q_buf, keys, values, visible, rows, out_buf, lane, local_kv, group_size, unroll):
     score_scale = HEAD ** (-0.5)
     count = rows.stop - rows.start
     tiled = jnp.concatenate([visible] * group_size, axis=0)
@@ -197,7 +197,7 @@
             out_buf[lane, :, h] = mixed[j * count : (j + 1) * count]
         return carry
 
-    lax.fori_loop(0, local_kv, attend_group, 0)
+    lax.fori_loop(0, local_kv, attend_group, 0, unroll=unroll)
 
 
 def fused_kernel(
@@ -230,10 +230,8 @@
     owner_ref,
     in_sem,
     w_sem,
-    k_send,
-    k_recv,
-    v_send,
-    v_recv,
+    kv_send,
+    kv_recv,
     p_send,
     p_recv,
     o_send,
@@ -247,7 +245,10 @@
     me = lax.axis_index("wide")
     lane = lax.axis_index("narrow")
     other = 1 - lane
-    peers = [lax.rem(me + k, wide_count) for k in range(1, wide_count)]
+    along, across = lax.rem(me, 2), me // 2
+    near = [across * 2 + 1 - along, (1 - across) * 2 + along]
+    far = (1 - across) * 2 + 1 - along
+    peers = [far] + near
     long_rows, short_rows = slice(0, rows), slice(rows, 2 * rows)
 
     barrier = pltpu.get_barrier_semaphore()
@@ -259,8 +260,8 @@
         pltpu.make_async_copy(q_hbm.at[pl.ds(rows, rows)], q_buf.at[pl.ds(rows, rows)], in_sem.at[0]),
         pltpu.make_async_copy(k_hbm.at[pl.ds(rows, rows)], ks_buf, in_sem.at[1]),
         pltpu.make_async_copy(v_hbm.at[pl.ds(rows, rows)], vs_buf, in_sem.at[2]),
-        pltpu.make_async_copy(seg_hbm, seg_ref, in_sem.at[6]),
     ]
+    seg_load = pltpu.make_async_copy(seg_hbm, seg_ref, in_sem.at[6])
     owner_load = pltpu.make_async_copy(owner_hbm, owner_ref, in_sem.at[7])
     gain_load = pltpu.make_async_copy(gain_hbm, gain_ref, in_sem.at[9])
     late_loads = [
@@ -276,30 +277,26 @@
         )
         for c in range(PIECES)
     ]
-    for load in loads + [owner_load] + w_loads + [res_load, gain_load] + late_loads:
+    for load in [owner_load, seg_load] + loads + w_loads + [res_load, gain_load] + late_loads:
         load.start()
 
-    pl.semaphore_wait(barrier, wide_count)
-
-    def kv_copy(source, peer):
-        return [
-            pltpu.make_async_remote_copy(
-                src_ref=hbm.at[pl.ds(0, rows)],
-                dst_ref=buf.at[source],
-                send_sem=send.at[peer],
-                recv_sem=recv.at[source],
-                device_id={"wide": peer},
-                device_id_type=MESH,
-            )
-            for hbm, buf, send, recv in (
-                (k_hbm, k_buf, k_send, k_recv),
-                (v_hbm, v_buf, v_send, v_recv),
-            )
-        ]
-
-    for peer in peers:
-        for copy in kv_copy(me, peer):
-            copy.start()
+    def kv_copy(i, source, peer, first, sem):
+        hbm, buf = ((k_hbm, k_buf), (v_hbm, v_buf))[i]
+        return pltpu.make_async_remote_copy(
+            src_ref=hbm.at[pl.ds(0, rows)] if first else buf.at[source],
+            dst_ref=buf.at[source],
+            send_sem=kv_send.at[i, sem],
+            recv_sem=kv_recv.at[i, source],
+            device_id={"wide": peer},
+            device_id_type=MESH,
+        )
+
+    kv_first = [kv_copy(i, me, near[j], True, j) for i in range(2) for j in range(2)]
+    kv_forward = [kv_copy(i, near[i], near[1 - i], False, 2) for i in range(2)]
+
+    def pass_on(i):
+        kv_copy(i, near[i], near[i], True, i).wait_recv()
+        kv_forward[i].start()
 
     row_id = lax.broadcasted_iota(jnp.int32, (rows, rows), 0)
     col_id = lax.broadcasted_iota(jnp.int32, (rows, rows), 1)
@@ -313,6 +310,14 @@
     slots = lax.broadcasted_iota(jnp.int32, (wide_count * capacity, rows), 0)
     dispatch = jnp.where(slots == target, 1.0, 0.0).astype(jnp.bfloat16)
 
+    seg_load.wait()
+    seg_across = jnp.broadcast_to(seg_ref[...], (rows, rows)).astype(jnp.float32)
+    short_visible = (seg_across == seg_across.T) & (col_id <= row_id)
+
+    pl.semaphore_wait(barrier, wide_count)
+    for copy in kv_first:
+        copy.start()
+
     def part_copy(c, phase):
         return pltpu.make_async_remote_copy(
             src_ref=part_buf.at[phase, c],
@@ -326,6 +331,10 @@
     def project(phase, c):
         if phase == 1:
             w_loads[c].wait()
+            if c == 2:
+                pass_on(0)
+            if c == 6:
+                pass_on(1)
         product = jnp.dot(att_buf[phase], w_buf[c], preferred_element_type=jnp.float32)
         part_buf[phase, c] = product.astype(jnp.bfloat16)
 
@@ -392,8 +401,6 @@
 
     for load in loads:
         load.wait()
-    seg_across = jnp.broadcast_to(seg_ref[...], (rows, rows)).astype(jnp.float32)
-    short_visible = (seg_across == seg_across.T) & (col_id <= row_id)
     attend_heads(
         q_buf,
         lambda group: ks_buf[:, group],
@@ -404,14 +411,16 @@
         1,
         local_kv,
         group_size,
+        True,
     )
     both(1)
 
     for load in late_loads:
         load.wait()
-    for peer in peers:
-        for copy in kv_copy(peer, peer):
-            copy.wait_recv()
+    kv_copy(0, near[1], near[1], True, 1).wait_recv()
+    kv_copy(1, near[0], near[0], True, 0).wait_recv()
+    for i in range(2):
+        kv_copy(i, far, near[1 - i], False, 2).wait_recv()
     spans = span_ref[...]
     wide_ids = lax.broadcasted_iota(jnp.int32, (1, wide_count), 1)
     own_span = jnp.sum(jnp.where(wide_ids == me, spans, 0), axis=1, keepdims=True)
@@ -432,12 +441,12 @@
         0,
         local_kv,
         group_size,
+        False,
     )
     both(0)
 
-    for peer in peers:
-        for copy in kv_copy(me, peer):
-            copy.wait_send()
+    for copy in kv_first + kv_forward:
+        copy.wait_send()
 
     def drain_parts(c, carry):
         part_copy(c, 0).wait_send()
@@ -518,10 +527,8 @@
             pltpu.VMEM((1, rows), jnp.int32),
             dma((11,)),
             dma((PIECES,)),
-            dma((wide_count,)),
-            dma((wide_count,)),
-            dma((wide_count,)),
-            dma((wide_count,)),
+            dma((2, 3)),
+            dma((2, wide_count)),
             dma((PIECES,)),
             dma((PIECES,)),
             dma((SENDS, wide_count)),
@@ -564,6 +571,7 @@
         lax.axis_size("narrow") == 2
         and rows == LONG_DEV
         and queries.shape[0] == 2 * LONG_DEV
+        and wide_count == 4
         and (2 * rows) % (32 * wide_count) == 0
         and rows % (16 * wide_count) == 0
         and model % (PIECES * HEAD) == 0

time: 37.5 us -> 39.6 us (1.056)
  Pallas kernels: 36.7 us -> 38.8 us
    pallas_call x1, Pallas kernels: 34.9 us -> 37.1 us  [fused_on_device(): pl.pallas_call(functools.partial(fused_kernel, sizes), out_shape=(pltpu.V...]
where the time goes in v6:
time: 39.6 us; the launch traced here: 39.5 us
  Pallas kernels  38.8 us (98%)
  between operations  0.64 us (2%)
    pallas_call x1, Pallas kernels, fused_on_device(): pl.pallas_call(functools.partial(fused_kernel, sizes), out_shape=(pltpu.V...  37.1 us
    pallas_call x1, Pallas kernels, fused_on_device(): pl.pallas_call(store_kernel, out_shape=(jax.ShapeDtypeStruct(hidden.shape...  1.76 us

profile of v6, /device:TPU:0, one launch (start us, length us, event | category | flops | bytes accessed | tf_op | source)
XLA Modules:
  0.0 39.5 jit_solution(11060866725870114866)
XLA Ops:
  0.6 37.1 %shard_map.104 = (bf16[128,4096]{1,0:T(8,128)(2,1)S(1)}, bf16[4,64,4096]{2,1,0:T(8,128)(2,1)S(1)}) custom-call(s32[1,4]{1,0:T(1,128)} %bitcast.5, s32[1,128]{1,0:T(1,128)} %seg_hbm.1, s32[1,128]{1,0:T(1,128)} %bitcast.6, bf16[256,1024]{1,0:T(8,128)(2,1)} %q_hbm.1, bf16[256,256]{1,0:T(8,128)(2,1)} %k_hbm.1, bf16[256,256]{1,0:T(8,128)(2,1)} %v_hbm.1, ...), custom_call_target="tpu_custom_call" | custom-call | tf_op jit(solution)/shard_map/pallas_call | solution.py:504
  37.7 1.8 %shard_map.105 = (bf16[128,4096]{1,0:T(8,128)(2,1)}, bf16[4,64,4096]{2,1,0:T(8,128)(2,1)}) custom-call(bf16[128,4096]{1,0:T(8,128)(2,1)S(1)} %get-tuple-element.6.hidden_ref, bf16[4,64,4096]{2,1,0:T(8,128)(2,1)S(1)} %get-tuple-element.7.ffn_ref), custom_call_target="tpu_custom_call" | custom-call | tf_op jit(solution)/shard_map/pallas_call | solution.py:552

commit v7 on v5

--- a/solution.py
+++ b/solution.py
@@ -166,6 +166,7 @@
 
 PIECES = 8
 SENDS = 4
+EARLY = 3
 MESH = pl.DeviceIdType.MESH
 
 
@@ -276,7 +277,7 @@
         )
         for c in range(PIECES)
     ]
-    for load in loads + [owner_load] + w_loads + [res_load, gain_load] + late_loads:
+    for load in loads + [owner_load] + w_loads[:EARLY]:
         load.start()
 
     pl.semaphore_wait(barrier, wide_count)
@@ -300,6 +301,8 @@
     for peer in peers:
         for copy in kv_copy(me, peer):
             copy.start()
+    for load in w_loads[EARLY:] + [res_load, gain_load] + late_loads:
+        load.start()
 
     row_id = lax.broadcasted_iota(jnp.int32, (rows, rows), 0)
     col_id = lax.broadcasted_iota(jnp.int32, (rows, rows), 1)

time: 37.5 us -> 37.5 us (level)
  no operation moved by 1% of the time
where the time goes in v7:
time: 37.5 us; the launch traced here: 37.3 us
  Pallas kernels  36.7 us (98%)
  between operations  0.64 us (2%)
    pallas_call x1, Pallas kernels, fused_on_device(): pl.pallas_call(functools.partial(fused_kernel, sizes), out_shape=(pltpu.V...  34.9 us
    pallas_call x1, Pallas kernels, fused_on_device(): pl.pallas_call(store_kernel, out_shape=(jax.ShapeDtypeStruct(hidden.shape...  1.76 us

profile of v7, /device:TPU:0, one launch (start us, length us, event | category | flops | bytes accessed | tf_op | source)
XLA Modules:
  0.0 37.3 jit_solution(18290743279438096070)
XLA Ops:
  0.6 34.9 %shard_map.104 = (bf16[128,4096]{1,0:T(8,128)(2,1)S(1)}, bf16[4,64,4096]{2,1,0:T(8,128)(2,1)S(1)}) custom-call(s32[1,4]{1,0:T(1,128)} %bitcast.5, s32[1,128]{1,0:T(1,128)} %seg_hbm.1, s32[1,128]{1,0:T(1,128)} %bitcast.6, bf16[256,1024]{1,0:T(8,128)(2,1)} %q_hbm.1, bf16[256,256]{1,0:T(8,128)(2,1)} %k_hbm.1, bf16[256,256]{1,0:T(8,128)(2,1)} %v_hbm.1, ...), custom_call_target="tpu_custom_call" | custom-call | tf_op jit(solution)/shard_map/pallas_call | solution.py:498
  35.6 1.8 %shard_map.105 = (bf16[128,4096]{1,0:T(8,128)(2,1)}, bf16[4,64,4096]{2,1,0:T(8,128)(2,1)}) custom-call(bf16[128,4096]{1,0:T(8,128)(2,1)S(1)} %get-tuple-element.6.hidden_ref, bf16[4,64,4096]{2,1,0:T(8,128)(2,1)S(1)} %get-tuple-element.7.ffn_ref), custom_call_target="tpu_custom_call" | custom-call | tf_op jit(solution)/shard_map/pallas_call | solution.py:548

commit v8 on v5

--- a/solution.py
+++ b/solution.py
@@ -166,10 +166,11 @@
 
 PIECES = 8
 SENDS = 4
+EARLY = 4
 MESH = pl.DeviceIdType.MESH
 
 
-def attend_heads(q_buf, keys, values, visible, rows, out_buf, lane, local_kv, group_size):
+def attend_heads(q_buf, keys, values, visible, rows, out_buf, lane, groups, group_size):
     score_scale = HEAD ** (-0.5)
     count = rows.stop - rows.start
     tiled = jnp.concatenate([visible] * group_size, axis=0)
@@ -197,7 +198,7 @@
             out_buf[lane, :, h] = mixed[j * count : (j + 1) * count]
         return carry
 
-    lax.fori_loop(0, local_kv, attend_group, 0)
+    lax.fori_loop(*groups, attend_group, 0)
 
 
 def fused_kernel(
@@ -276,10 +277,8 @@
         )
         for c in range(PIECES)
     ]
-    for load in loads + [owner_load] + w_loads + [res_load, gain_load] + late_loads:
+    for load in loads + [owner_load] + w_loads[:EARLY]:
         load.start()
-
-    pl.semaphore_wait(barrier, wide_count)
 
     def kv_copy(source, peer):
         return [
@@ -296,10 +295,6 @@
                 (v_hbm, v_buf, v_send, v_recv),
             )
         ]
-
-    for peer in peers:
-        for copy in kv_copy(me, peer):
-            copy.start()
 
     row_id = lax.broadcasted_iota(jnp.int32, (rows, rows), 0)
     col_id = lax.broadcasted_iota(jnp.int32, (rows, rows), 1)
@@ -394,17 +389,29 @@
         load.wait()
     seg_across = jnp.broadcast_to(seg_ref[...], (rows, rows)).astype(jnp.float32)
     short_visible = (seg_across == seg_across.T) & (col_id <= row_id)
-    attend_heads(
-        q_buf,
-        lambda group: ks_buf[:, group],
-        lambda group: vs_buf[:, group],
-        short_visible,
-        short_rows,
-        att_buf,
-        1,
-        local_kv,
-        group_size,
-    )
+
+    def attend_short(first, last):
+        attend_heads(
+            q_buf,
+            lambda group: ks_buf[:, group],
+            lambda group: vs_buf[:, group],
+            short_visible,
+            short_rows,
+            att_buf,
+            1,
+            (first, last),
+            group_size,
+        )
+
+    attend_short(0, 1)
+    pl.semaphore_wait(barrier, wide_count)
+    for peer in peers:
+        for copy in kv_copy(me, peer):
+            copy.start()
+    for load in w_loads[EARLY:] + [res_load, gain_load] + late_loads:
+        load.start()
+
+    attend_short(1, local_kv)
     both(1)
 
     for load in late_loads:
@@ -430,7 +437,7 @@
         long_rows,
         att_buf,
         0,
-        local_kv,
+        (0, local_kv),
         group_size,
     )
     both(0)

time: 37.5 us -> 37.9 us (1.011)
  Pallas kernels: 36.7 us -> 37.1 us
    pallas_call x1, Pallas kernels: 34.9 us -> 35.4 us  [fused_on_device(): pl.pallas_call(functools.partial(fused_kernel, sizes), out_shape=(pltpu.V...]
where the time goes in v8:
time: 37.9 us; the launch traced here: 37.8 us
  Pallas kernels  37.1 us (98%)
  between operations  0.64 us (2%)
    pallas_call x1, Pallas kernels, fused_on_device(): pl.pallas_call(functools.partial(fused_kernel, sizes), out_shape=(pltpu.V...  35.4 us
    pallas_call x1, Pallas kernels, fused_on_device(): pl.pallas_call(store_kernel, out_shape=(jax.ShapeDtypeStruct(hidden.shape...  1.76 us

profile of v8, /device:TPU:0, one launch (start us, length us, event | category | flops | bytes accessed | tf_op | source)
XLA Modules:
  0.0 37.8 jit_solution(8728115363813670799)
XLA Ops:
  0.6 35.4 %shard_map.104 = (bf16[128,4096]{1,0:T(8,128)(2,1)S(1)}, bf16[4,64,4096]{2,1,0:T(8,128)(2,1)S(1)}) custom-call(s32[1,4]{1,0:T(1,128)} %bitcast.5, s32[1,128]{1,0:T(1,128)} %seg_hbm.1, s32[1,128]{1,0:T(1,128)} %bitcast.6, bf16[256,1024]{1,0:T(8,128)(2,1)} %q_hbm.1, bf16[256,256]{1,0:T(8,128)(2,1)} %k_hbm.1, bf16[256,256]{1,0:T(8,128)(2,1)} %v_hbm.1, ...), custom_call_target="tpu_custom_call" | custom-call | tf_op jit(solution)/shard_map/pallas_call | solution.py:502
  36.0 1.8 %shard_map.105 = (bf16[128,4096]{1,0:T(8,128)(2,1)}, bf16[4,64,4096]{2,1,0:T(8,128)(2,1)}) custom-call(bf16[128,4096]{1,0:T(8,128)(2,1)S(1)} %get-tuple-element.6.hidden_ref, bf16[4,64,4096]{2,1,0:T(8,128)(2,1)S(1)} %get-tuple-element.7.ffn_ref), custom_call_target="tpu_custom_call" | custom-call | tf_op jit(solution)/shard_map/pallas_call | solution.py:552

commit v9 on v7

--- a/solution.py
+++ b/solution.py
@@ -198,7 +198,7 @@
             out_buf[lane, :, h] = mixed[j * count : (j + 1) * count]
         return carry
 
-    lax.fori_loop(0, local_kv, attend_group, 0)
+    lax.fori_loop(0, local_kv, attend_group, 0, unroll=True)
 
 
 def fused_kernel(

time: 37.5 us -> 37.2 us (level)
  no operation moved by 1% of the time
where the time goes in v9:
time: 37.2 us; the launch traced here: 37 us
  Pallas kernels  36.4 us (98%)
  between operations  0.64 us (2%)
    pallas_call x1, Pallas kernels, fused_on_device(): pl.pallas_call(functools.partial(fused_kernel, sizes), out_shape=(pltpu.V...  34.6 us
    pallas_call x1, Pallas kernels, fused_on_device(): pl.pallas_call(store_kernel, out_shape=(jax.ShapeDtypeStruct(hidden.shape...  1.76 us

profile of v9, /device:TPU:0, one launch (start us, length us, event | category | flops | bytes accessed | tf_op | source)
XLA Modules:
  0.0 37.0 jit_solution(17237514745126650531)
XLA Ops:
  0.6 34.6 %shard_map.104 = (bf16[128,4096]{1,0:T(8,128)(2,1)S(1)}, bf16[4,64,4096]{2,1,0:T(8,128)(2,1)S(1)}) custom-call(s32[1,4]{1,0:T(1,128)} %bitcast.5, s32[1,128]{1,0:T(1,128)} %seg_hbm.1, s32[1,128]{1,0:T(1,128)} %bitcast.6, bf16[256,1024]{1,0:T(8,128)(2,1)} %q_hbm.1, bf16[256,256]{1,0:T(8,128)(2,1)} %k_hbm.1, bf16[256,256]{1,0:T(8,128)(2,1)} %v_hbm.1, ...), custom_call_target="tpu_custom_call" | custom-call | tf_op jit(solution)/shard_map/pallas_call | solution.py:498
  35.3 1.8 %shard_map.105 = (bf16[128,4096]{1,0:T(8,128)(2,1)}, bf16[4,64,4096]{2,1,0:T(8,128)(2,1)}) custom-call(bf16[128,4096]{1,0:T(8,128)(2,1)S(1)} %get-tuple-element.6.hidden_ref, bf16[4,64,4096]{2,1,0:T(8,128)(2,1)S(1)} %get-tuple-element.7.ffn_ref), custom_call_target="tpu_custom_call" | custom-call | tf_op jit(solution)/shard_map/pallas_call | solution.py:548
